TPU v7x, 256 devices: a whole 4x4x8 slice. The times are simulated.
256 devices in a mesh: seq: 32 (over x, z), head: 8 (over y, core).
Axes of the slice: x: 4, y: 4, z: 8, core: 2. Of those that a mesh axis runs over, the one named last changes fastest.
Arguments:
- attn_queries: bfloat16 [16384, 16, 128], P('seq', 'head'), may hold values from -20 to 20
- attn_keys: bfloat16 [16384, 16, 128], P('seq', 'head'), may hold values from -20 to 20
- attn_values: bfloat16 [16384, 16, 128], P('seq', 'head'), may hold values from -6 to 6
- attn_out_grad: bfloat16 [16384, 16, 128], P('seq', 'head'), may hold values from -6 to 6
- ssm_input: bfloat16 [16384, 8192], P('seq', 'head'), may hold values from -6 to 6
- log_decay: float32 [16384, 128], P('seq', 'head'), may hold values from -1 to 0
- b_proj: bfloat16 [16384, 128], P('seq'), may hold values from -0.5 to 0.5
- c_proj: bfloat16 [16384, 128], P('seq'), may hold values from -0.5 to 0.5
- ssm_out_grad: bfloat16 [16384, 8192], P('seq', 'head'), may hold values from -0.29882812 to 0.29882812
- global_owner: int32 [128, 4], replicated, may hold values from 0 to 31, all different within a row; in each aligned block of 4 rows (0 to 3, 4 to 7, ...) at most 2 rows name the same one
- global_offset: int32 [128, 4], replicated, may hold values from 0 to 3
- global_count: int32 [128], replicated, may hold values from 3 to 4
Outputs:
- query_grad: bfloat16 [16384, 16, 128], P('seq', 'head')
- key_grad: bfloat16 [16384, 16, 128], P('seq', 'head')
- value_grad: bfloat16 [16384, 16, 128], P('seq', 'head')
- input_grad: bfloat16 [16384, 8192], P('seq', 'head')
- decay_grad: float32 [16384, 128], P('seq', 'head')
- b_grad: float32 [16384, 128], P('seq')
- c_grad: float32 [16384, 128], P('seq')
Inputs may be any that keep to these rules, and one draw needn't show every extreme that they name: `global_owner`: in every aligned block of 4 rows (the query blocks of one index of seq) no index is named by more than 2 rows, and the 4 entries of a row differ. Only the first global_count[q] entries of row q of global_owner and global_offset are listed.
All inputs are finite; a program needn't handle non-finite values.
Results may differ from a plain program's by a relative error of at most 0.017.
Values may be sent and summed in bfloat16 or wider, within the bound.
No kernel may reach another device: no remote copies, remote signals or barrier semaphores. Data moves between devices by JAX's collectives and lax.ppermute only.
A program may use at most 192 MiB of HBM per device.

v0:
```python
import functools
import math

import jax
import jax.numpy as jnp
from jax import lax
from jax.experimental import pallas as pl
from jax.experimental.pallas import tpu as pltpu
from jax.sharding import PartitionSpec as P

HD = 128
HP = 64
NST = 128
BLK = 128
STRETCH = 128
SEG = 4
GLOB = 4
TOK = 512
SH = 16
WIDTH = SH * HP
ITEMS = SEG * GLOB
NX = 4
NZ = 8
NS = NX * NZ
ROWS = WIDTH // NS
PAY = 2 * ROWS + 16
STRETCHES = TOK // STRETCH

HIGH = lax.Precision.HIGHEST
F32 = jnp.float32
BF16 = jnp.bfloat16
Z_GROUPS = [[x * NZ + z for z in range(NZ)] for x in range(NX)]
X_GROUPS = [[x * NZ + z for x in range(NX)] for z in range(NZ)]


def dot(a, b, dims, precision=None):
    return lax.dot_general(
        a, b, (dims, ((), ())), precision=precision, preferred_element_type=F32
    )


def mm(a, b):
    return dot(a, b, ((1,), (0,)))


def mm_nt(a, b):
    return dot(a, b, ((1,), (1,)))


def mm_tn(a, b):
    return dot(a, b, ((0,), (0,)))


def call(body, name, outs, ins, scratch, flops, nbytes, vmem=48 << 20):
    return pl.pallas_call(
        body,
        out_shape=[jax.ShapeDtypeStruct(s, d) for s, d, _ in outs],
        in_specs=[pl.BlockSpec(memory_space=m) for m in ins],
        out_specs=[pl.BlockSpec(memory_space=m) for _, _, m in outs],
        scratch_shapes=scratch,
        compiler_params=pltpu.CompilerParams(vmem_limit_bytes=vmem),
        cost_estimate=pl.CostEstimate(flops=flops, bytes_accessed=nbytes, transcendentals=0),
        name=name,
    )


SCALE = 1.0 / math.sqrt(HD)
EMPTY = -1e30
KINDS = 3
FAR = NZ * SEG


def list_items(codes, me, places, blocks):
    here = me[0]
    my_x = here >> 3
    my_z = here & (NZ - 1)
    count = jnp.int32(0)
    for d in range(NX):
        base = (((my_x - d) & (NX - 1)) * NZ + my_z) * ITEMS

        def item(i, n, d=d, base=base):
            code = codes[base + i]
            places[n] = code & (FAR - 1)
            blocks[n] = d * SEG + (i >> 2)
            return n + ((code >= 0) & ((code >> 5) == my_x)).astype(jnp.int32)

        count = lax.fori_loop(0, ITEMS, item, count)
    places[count] = 0
    blocks[count] = NX * SEG
    return count


def span(index):
    return pl.ds(pl.multiple_of(index * BLK, BLK), BLK)


def pairs(count, visit):
    def two(t, _):
        visit([2 * t, 2 * t + 1])
        return 0

    lax.fori_loop(0, (count + 1) >> 1, two, 0)


def fetch(qos, keys, place, block):
    d = jnp.minimum(block >> 2, NX - 1)
    rows = span(block & (SEG - 1))
    z = place >> 2
    cols = span(place & (SEG - 1))
    return [
        (qos[d, h, 0, rows, :], qos[d, h, 1, rows, :], keys[z, h, 0, cols, :], keys[z, h, 1, cols, :])
        for h in range(2)
    ]


def summary(q, o, k, v):
    s = mm_nt(k, q) * SCALE
    dp = mm_nt(v, o)
    m = jnp.max(s, axis=0, keepdims=True)
    e = jnp.exp(s - m)
    return m, jnp.sum(e, axis=0, keepdims=True), jnp.sum(e * dp, axis=0, keepdims=True)


def stack_rows(rows):
    return jnp.concatenate(rows + [jnp.zeros((8 - len(rows), rows[0].shape[1]), F32)], axis=0)


def near_stats_body(qo, kv, out):
    for b in range(SEG):
        rows = pl.ds(b * BLK, BLK)
        parts = []
        for h in range(2):
            parts += summary(qo[h, 0, rows, :], qo[h, 1, rows, :], kv[h, 0], kv[h, 1])
        out[:, rows] = stack_rows(parts)


def near_stats(qo, kv):
    vm = pltpu.VMEM
    return call(
        near_stats_body,
        "near_stats",
        [((8, TOK), F32, vm)],
        [vm, vm],
        [],
        2 * 2 * 2 * TOK * TOK * HD,
        1 << 20,
    )(qo, kv)[0]


def far_stats_body(codes, me, near, column, qos, out, tally, places, blocks):
    count = list_items(codes, me, places, blocks)
    kind = lax.broadcasted_iota(jnp.int32, (8, BLK), 0)
    start = jnp.where((kind == 0) | (kind == KINDS), EMPTY, 0.0)
    for n in range(NX * SEG + 1):
        tally[n] = start

    def visit(items):
        found = []
        for n in items:
            found.append([summary(*part) for part in fetch(qos, column, places[n], blocks[n])])
        for n, heads in zip(items, found):
            old = tally[blocks[n]]
            rows = []
            for h, (m, l, t) in enumerate(heads):
                m0, l0, t0 = [old[KINDS * h + i : KINDS * h + i + 1, :] for i in range(KINDS)]
                high = jnp.maximum(m0, m)
                f0 = jnp.exp(m0 - high)
                f1 = jnp.exp(m - high)
                rows += [high, l0 * f0 + l * f1, t0 * f0 + t * f1]
            tally[blocks[n]] = stack_rows(rows)

    pairs(count, visit)
    for d in range(NX):
        for b in range(SEG):
            out[d, :, pl.ds(b * BLK, BLK)] = tally[d * SEG + b]
    out[NX] = near[...]


def item_scratch():
    return [pltpu.SMEM((NX * ITEMS + 1,), jnp.int32)] * 2


def far_stats(codes, me, near, column, qos):
    vm = pltpu.VMEM
    return call(
        far_stats_body,
        "far_stats",
        [((NX + 1, 8, TOK), F32, vm)],
        [pltpu.SMEM, pltpu.SMEM] + [vm] * 3,
        [vm((NX * SEG + 1, 8, BLK), F32)] + item_scratch(),
        2 * 2 * 2 * 16 * BLK * BLK * HD,
        6 << 20,
    )(codes, me, near, column, qos)[0]


def joined(stats, my_x, x_q):
    parts = []
    for r in range(NX):
        x = (my_x - r) & (NX - 1)
        parts.append(stats[r, (x - x_q) & (NX - 1)])
    parts.append(stats[(my_x - x_q) & (NX - 1), NX])
    rows = []
    for h in range(2):
        at = KINDS * h
        high = functools.reduce(jnp.maximum, [p[at : at + 1, :] for p in parts])
        fade = [jnp.exp(p[at : at + 1, :] - high) for p in parts]
        total = sum(f * p[at + 1 : at + 2, :] for f, p in zip(fade, parts))
        mixed = sum(f * p[at + 2 : at + 3, :] for f, p in zip(fade, parts))
        inverse = 1.0 / total
        rows += [high, inverse, mixed * inverse]
    return stack_rows(rows)


def weights_of(q, o, k, v, row):
    high, inverse, delta = [row[i : i + 1, :] for i in range(KINDS)]
    p = jnp.exp(mm_nt(k, q) * SCALE - high) * inverse
    ds = (p * (mm_nt(v, o) - delta) * SCALE).astype(BF16)
    return p.astype(BF16), ds


def far_grads_body(
    codes, me, stats, column, qos, kv_out, dq_out, total, dq, rowed, places, blocks
):
    my_x = me[0] >> 3
    count = list_items(codes, me, places, blocks)
    total[...] = jnp.zeros_like(total)
    dq[...] = jnp.zeros_like(dq)
    for d in range(NX):
        row = joined(stats, my_x, (my_x - d) & (NX - 1))
        for b in range(SEG):
            rowed[d * SEG + b] = row[:, b * BLK : (b + 1) * BLK]
    rowed[NX * SEG] = jnp.zeros((8, BLK), F32)

    def visit(items):
        found = []
        for n in items:
            row = rowed[blocks[n]]
            heads = fetch(qos, column, places[n], blocks[n])
            grads = []
            for h, (q, o, k, v) in enumerate(heads):
                p, ds = weights_of(q, o, k, v, row[KINDS * h : KINDS * h + KINDS, :])
                grads.append((mm_tn(ds, k), mm(ds, q), mm(p, o)))
            found.append(grads)
        for n, grads in zip(items, found):
            at = blocks[n]
            to = jnp.where(at == NX * SEG, FAR, places[n])
            for h, (dqh, dkh, dvh) in enumerate(grads):
                dq[at, h] += dqh
                total[to, h, 0] += dkh
                total[to, h, 1] += dvh

    pairs(count, visit)
    for d in range(NX):
        for b in range(SEG):
            dq_out[(my_x - d) & (NX - 1), :, pl.ds(b * BLK, BLK), :] = dq[d * SEG + b].astype(BF16)
    for z in range(NZ):
        for h in range(2):
            for s in range(2):
                for b in range(SEG):
                    at = (2 * h + s) * TOK + b * BLK
                    kv_out[z, pl.ds(at, BLK), :] = total[z * SEG + b, h, s].astype(BF16)


def far_grads(codes, me, stats, column, qos):
    vm = pltpu.VMEM
    return call(
        far_grads_body,
        "far_grads",
        [((NZ, 4 * TOK, HD), BF16, vm), ((NX, 2, TOK, HD), BF16, vm)],
        [pltpu.SMEM, pltpu.SMEM] + [vm] * 3,
        [
            vm((FAR + 1, 2, 2, BLK, HD), F32),
            vm((NX * SEG + 1, 2, BLK, HD), F32),
            vm((NX * SEG + 1, 8, BLK), F32),
        ]
        + item_scratch(),
        5 * 2 * 2 * 16 * BLK * BLK * HD,
        12 << 20,
    )(codes, me, stats, column, qos)


def near_grads_body(me, stats, qo, kv, dq_out, kv_out, p_keep, s_keep):
    my_x = me[0] >> 3
    row = joined(stats, my_x, my_x)
    for h in range(2):
        k = kv[h, 0]
        for b in range(SEG):
            rows = pl.ds(b * BLK, BLK)
            p, ds = weights_of(
                qo[h, 0, rows, :], qo[h, 1, rows, :], k, kv[h, 1],
                row[KINDS * h : KINDS * h + KINDS, b * BLK : (b + 1) * BLK],
            )
            dq_out[h, rows, :] = mm_tn(ds, k)
            p_keep[:, rows] = p
            s_keep[:, rows] = ds
        kv_out[h, 0] = mm(s_keep[...], qo[h, 0])
        kv_out[h, 1] = mm(p_keep[...], qo[h, 1])


def near_grads(me, stats, qo, kv):
    vm = pltpu.VMEM
    return call(
        near_grads_body,
        "near_grads",
        [((2, TOK, HD), F32, vm), ((2, 2, TOK, HD), F32, vm)],
        [pltpu.SMEM] + [vm] * 3,
        [vm((TOK, TOK), BF16), vm((TOK, TOK), BF16)],
        5 * 2 * 2 * TOK * TOK * HD,
        4 << 20,
    )(me, stats, qo, kv)


def triangle(lower):
    i = lax.broadcasted_iota(jnp.int32, (STRETCH, STRETCH), 0)
    j = lax.broadcasted_iota(jnp.int32, (STRETCH, STRETCH), 1)
    return i >= j if lower else i <= j


def head_map(transposed):
    shape = (WIDTH, SH) if transposed else (SH, WIDTH)
    wide = lax.broadcasted_iota(jnp.int32, shape, 0 if transposed else 1)
    head = lax.broadcasted_iota(jnp.int32, shape, 1 if transposed else 0)
    return ((wide >> 6) == head).astype(BF16)


def two_part(a, b):
    high = a.astype(BF16)
    low = (a - high.astype(F32)).astype(BF16)
    return mm(high, b) + mm(low, b)


def per_head(rates, state):
    return jnp.concatenate(
        [state[h * HP : (h + 1) * HP, :] * rates[0:1, h : h + 1] for h in range(SH)], axis=0
    )


def ends_body(x_ref, g_ref, ld_ref, b_ref, c_ref, ends, starts, pay):
    lower = triangle(True).astype(F32)
    spread = head_map(False)
    last = []
    for k in range(STRETCHES):
        rows = pl.ds(k * STRETCH, STRETCH)
        cumul = dot(lower, ld_ref[rows, :], ((1,), (0,)), HIGH)
        tot = cumul[STRETCH - 1 : STRETCH, :]
        last.append(tot)
        tail = two_part(jnp.exp(tot - cumul), spread)
        lead = two_part(jnp.exp(cumul), spread)
        x_in = (x_ref[rows, :].astype(F32) * tail).astype(BF16)
        g_in = (g_ref[rows, :].astype(F32) * lead).astype(BF16)
        ends[k] = mm_tn(x_in, b_ref[rows, :])
        starts[k] = mm_tn(g_in, c_ref[rows, :])
    rates = [jnp.exp(t) for t in last]
    state = ends[0]
    for k in range(1, STRETCHES):
        state = per_head(rates[k], state) + ends[k]
    pay[:, 0:ROWS, :] = state.astype(BF16).reshape(NS, ROWS, NST)
    grad = starts[STRETCHES - 1]
    for k in range(STRETCHES - 2, -1, -1):
        grad = per_head(rates[k], grad) + starts[k]
    pay[:, ROWS : 2 * ROWS, :] = grad.astype(BF16).reshape(NS, ROWS, NST)
    whole = functools.reduce(jnp.add, last)
    high = whole.astype(BF16).astype(F32)
    low = whole - high
    line = lax.broadcasted_iota(jnp.int32, (16, NST), 0)
    for r in range(NS):
        h = r // 2
        a = jnp.broadcast_to(high[0:1, h : h + 1], (16, NST))
        b = jnp.broadcast_to(low[0:1, h : h + 1], (16, NST))
        pay[r, 2 * ROWS : PAY, :] = jnp.where(
            line == 0, a, jnp.where(line == 1, b, 0.0)
        ).astype(BF16)


def scan_ends(x, g, ld, b, c):
    vm = pltpu.VMEM
    return call(
        ends_body,
        "scan_ends",
        [
            ((STRETCHES, WIDTH, NST), F32, vm),
            ((STRETCHES, WIDTH, NST), F32, vm),
            ((NS, PAY, NST), BF16, vm),
        ],
        [vm] * 5,
        [],
        2 * 2 * TOK * WIDTH * NST * 4,
        8 << 20,
    )(x, g, ld, b, c)


def prefix_body(inp, out):
    def forward(j, state):
        out[j, 0:ROWS, :] = state.astype(BF16)
        rest = inp[j, 2 * ROWS : PAY, :].astype(F32)
        rate = jnp.exp(rest[0:1, :] + rest[1:2, :])
        return rate * state + inp[j, 0:ROWS, :].astype(F32)

    def backward(t, grad):
        j = NS - 1 - t
        out[j, ROWS : 2 * ROWS, :] = grad.astype(BF16)
        rest = inp[j, 2 * ROWS : PAY, :].astype(F32)
        rate = jnp.exp(rest[0:1, :] + rest[1:2, :])
        return rate * grad + inp[j, ROWS : 2 * ROWS, :].astype(F32)

    zero = jnp.zeros((ROWS, NST), F32)
    lax.fori_loop(0, NS, forward, zero)
    lax.fori_loop(0, NS, backward, zero)


def scan_prefix(inp):
    vm = pltpu.VMEM
    return call(
        prefix_body,
        "scan_prefix",
        [((NS, 2 * ROWS, NST), BF16, vm)],
        [vm],
        [],
        0,
        2 << 20,
    )(inp)[0]


def grads_body(
    x_ref, g_ref, ld_ref, b_ref, c_ref, ends, starts, carried, dx_ref, dl_ref, bc_ref,
    states, grads, y_keep, d_keep,
):
    lower_mask = triangle(True)
    lower = lower_mask.astype(F32)
    upper = triangle(False).astype(F32)
    spread = head_map(False)
    gathered = head_map(True)
    ones = jnp.ones((8, NST), F32)
    rates = []
    for k in range(STRETCHES):
        ld = ld_ref[pl.ds(k * STRETCH, STRETCH), :]
        rates.append(jnp.exp(jnp.sum(ld, axis=0, keepdims=True)))
    state = carried[:, 0:ROWS, :].reshape(WIDTH, NST).astype(F32)
    states[0] = state.astype(BF16)
    for k in range(STRETCHES):
        state = per_head(rates[k], state) + ends[k]
        states[k + 1] = state.astype(BF16)
    grad = carried[:, ROWS : 2 * ROWS, :].reshape(WIDTH, NST).astype(F32)
    grads[STRETCHES - 1] = grad.astype(BF16)
    for k in range(STRETCHES - 1, 0, -1):
        grad = per_head(rates[k], grad) + starts[k]
        grads[k - 1] = grad.astype(BF16)

    def stretch(k, _):
        rows = pl.ds(pl.multiple_of(k * STRETCH, STRETCH), STRETCH)
        ld = ld_ref[rows, :]
        cumul = dot(lower, ld, ((1,), (0,)), HIGH)
        cumul_t = dot(ld, upper, ((0,), (0,)), HIGH)
        tot = cumul[STRETCH - 1 : STRETCH, :]
        b = b_ref[rows, :]
        c = c_ref[rows, :]
        cb = jnp.where(lower_mask, mm_nt(c, b), 0.0)
        mixed = jnp.zeros((STRETCH, STRETCH), F32)
        for h in range(SH):
            cols = pl.ds(h * HP, HP)
            x_h = x_ref[rows, cols]
            g_h = g_ref[rows, cols]
            gap = jnp.minimum(cumul[:, h : h + 1] - cumul_t[h : h + 1, :], 0.0)
            decay = jnp.exp(gap)
            weight = (decay * cb).astype(BF16)
            mixed = mixed + decay * mm_nt(g_h, x_h)
            y_keep[:, cols] = mm(weight, x_h)
            d_keep[:, cols] = mm_tn(weight, g_h)
        mixed = jnp.where(lower_mask, mixed, 0.0).astype(BF16)
        state = states[k]
        grad = grads[k]
        lead = two_part(jnp.exp(cumul), spread)
        tail = two_part(jnp.exp(tot - cumul), spread)
        x = x_ref[rows, :].astype(F32)
        g = g_ref[rows, :].astype(F32)
        y = y_keep[...] + lead * mm_nt(c, state)
        d = d_keep[...] + tail * mm_nt(b, grad)
        dx_ref[rows, :] = d.astype(BF16)
        bc_ref[rows, :] = (mm_tn(mixed, c) + mm((tail * x).astype(BF16), grad)).astype(BF16)
        c_rows = pl.ds(pl.multiple_of(TOK + k * STRETCH, STRETCH), STRETCH)
        bc_ref[c_rows, :] = (mm(mixed, b) + mm((lead * g).astype(BF16), state)).astype(BF16)
        change = two_part(g * y - x * d, gathered)
        meet = grad.astype(F32) * states[k + 1].astype(F32)
        meet = jnp.sum(meet.reshape(SH, HP, NST), axis=1)
        edge = dot(ones, meet, ((1,), (1,)), HIGH)[0:1, :]
        dl_ref[rows, :] = dot(upper, change, ((1,), (0,)), HIGH) + edge
        return 0

    lax.fori_loop(0, STRETCHES, stretch, 0)


def scan_grads(x, g, ld, b, c, ends, starts, carried):
    vm = pltpu.VMEM
    return call(
        grads_body,
        "scan_grads",
        [
            ((TOK, WIDTH), BF16, vm),
            ((TOK, SH), F32, vm),
            ((2 * TOK, NST), BF16, vm),
        ],
        [vm] * 8,
        [
            vm((STRETCHES + 1, WIDTH, NST), BF16),
            vm((STRETCHES, WIDTH, NST), BF16),
            vm((STRETCH, WIDTH), F32),
            vm((STRETCH, WIDTH), F32),
        ],
        2 * 8 * TOK * WIDTH * NST * 4,
        12 << 20,
    )(x, g, ld, b, c, ends, starts, carried)


def exchange(value, groups=None):
    return lax.all_to_all(value, "seq", 0, 0, tiled=True, axis_index_groups=groups)


def along_x(value, step):
    pairs = [
        (x * NZ + z, (x + step) % NX * NZ + z) for x in range(NX) for z in range(NZ)
    ]
    return lax.ppermute(value, "seq", pairs)


def after(value, *earlier):
    return lax.optimization_barrier((value, earlier))[0]


def per_device(q, k, v, o, x, ld, b, c, g, owner, offset, count):
    me = lax.axis_index("seq").astype(jnp.int32).reshape(1)
    live = jnp.arange(GLOB)[None, :] < count[:, None]
    codes = jnp.where(live, owner * SEG + offset, -1).reshape(NS * ITEMS)
    heads = range(q.shape[1])
    kv = jnp.stack([jnp.stack([k[:, h], v[:, h]]) for h in heads])
    qo = jnp.stack([jnp.stack([q[:, h], o[:, h]]) for h in heads])
    column = lax.all_gather(kv, "seq", axis_index_groups=Z_GROUPS)
    qos = jnp.stack([qo] + [along_x(qo, d) for d in range(1, NX)])
    near = near_stats(qo, kv)
    ends, starts, pay = scan_ends(x, g, ld, b, c)
    pay = exchange(after(pay, qos))
    carried = exchange(scan_prefix(after(pay, column)))
    column = after(column, pay)
    stats = far_stats(codes, me, near, column, qos)
    stats = jnp.stack([stats] + [along_x(stats, d) for d in range(1, NX)])
    stats = after(stats, carried)
    kv_far, dq_far = far_grads(codes, me, stats, column, qos)
    kv_far = lax.psum_scatter(
        kv_far, "seq", scatter_dimension=0, axis_index_groups=Z_GROUPS
    )
    carried = after(carried, dq_far)
    dq_far = exchange(dq_far, X_GROUPS)
    dx, dl, bc = scan_grads(x, g, ld, b, c, ends, starts, carried)
    shares = lax.all_to_all(bc.reshape(8, 128, NST), "head", 0, 0, tiled=True)
    part = jnp.sum(shares.astype(F32), axis=0).astype(BF16)
    whole = lax.all_gather(part, "head", tiled=True).astype(F32)
    dq_near, kv_near = near_grads(me, after(stats, dq_far), qo, kv)
    dq = (dq_near + jnp.sum(dq_far.astype(F32), axis=0)).astype(BF16)
    kv_grad = (kv_near + kv_far.astype(F32).reshape(kv_near.shape)).astype(BF16)
    return (
        jnp.swapaxes(dq, 0, 1),
        jnp.swapaxes(kv_grad[:, 0], 0, 1),
        jnp.swapaxes(kv_grad[:, 1], 0, 1),
        dx,
        dl,
        whole[:TOK],
        whole[TOK:],
    )


def solution(mesh):
    wide = P("seq", "head", None)
    flat = P("seq", "head")
    own = P("seq", None)
    return jax.shard_map(
        per_device,
        mesh=mesh,
        in_specs=(wide, wide, wide, wide, flat, flat, own, own, flat, P(), P(), P()),
        out_specs=(wide, wide, wide, flat, flat, own, own),
        check_vma=False,
    )
```

profile of v0, /device:TPU:1, one launch (start us, length us, event | category | flops | bytes accessed | tf_op | source)
XLA Modules:
  0.0 191.9 jit_solution(15959339970600126856)
XLA Ops:
  7.2 1.5 fusion.4
  8.7 1.5 fusion.5
  13.1 3.3 %collective-permute-start.2 = (bf16[2,2,512,128]{3,2,1,0:T(8,128)(2,1)S(1)}, bf16[2,2,512,128]{3,2,1,0:T(8,128)(2,1)}, u32[]{:S(2)}, u32[]{:S(2)}) collective-permute-start(bf16[2,2,512,128]{3,2,1,0:T(8,128)(2,1)S(1)} %get-tuple-element.63.qo), channel_id=1, source_target_pairs={{0,192},{8,200},{16,208},{24,216},{32,224},{40,232},{48,240},{56,2... | collective-permute-start | bytes 1572872 | tf_op jit(solution)/shard_map/ppermute | solution.py:522
  17.8 4.4 %scan_ends.1 = (f32[4,1024,128]{2,1,0:T(8,128)S(1)}, f32[4,1024,128]{2,1,0:T(8,128)}, bf16[32,80,128]{2,1,0:T(8,128)(2,1)S(1)}) custom-call(bf16[512,1024]{1,0:T(8,128)(2,1)S(1)} %copy-done.7, bf16[512,1024]{1,0:T(8,128)(2,1)S(1)} %copy-done.9, f32[512,16]{1,0:T(8,128)S(1)} %copy.57.ld_ref, bf16[512,128]{1,0:T(8,128)(2,1)S(1)} %copy-done.11, ...), custom_call_target="tpu_custom_call" | custom-call | flops 1073741824 | bytes 8388608 | tf_op jit(solution)/shard_map/scan_ends/pallas_call | solution.py:377
  22.2 7.9 %collective-permute-done.2 = bf16[2,2,512,128]{3,2,1,0:T(8,128)(2,1)} collective-permute-done((bf16[2,2,512,128]{3,2,1,0:T(8,128)(2,1)S(1)}, bf16[2,2,512,128]{3,2,1,0:T(8,128)(2,1)}, u32[]{:S(2)}, u32[]{:S(2)}) %collective-permute-start.2) | collective-permute-done | bytes 524320 | tf_op jit(solution)/shard_map/ppermute | solution.py:522
  30.6 12.6 %collective-permute-done = bf16[2,2,512,128]{3,2,1,0:T(8,128)(2,1)} collective-permute-done((bf16[2,2,512,128]{3,2,1,0:T(8,128)(2,1)S(1)}, bf16[2,2,512,128]{3,2,1,0:T(8,128)(2,1)}, u32[]{:S(2)}, u32[]{:S(2)}) %collective-permute-start) | collective-permute-done | bytes 524320 | tf_op jit(solution)/shard_map/ppermute | solution.py:522
  43.1 1.6 pad_maximum_fusion.qos
  44.8 33.5 %all_to_all.20.inp = bf16[32,80,128]{2,1,0:T(8,128)(2,1)S(1)} all-to-all(bf16[32,80,128]{2,1,0:T(8,128)(2,1)S(1)} %get-tuple-element.24), channel_id=1, replica_groups=mesh['seq'=32,'head'=8] {'seq'}, dimensions={0} | all-to-all | bytes 1310720 | tf_op jit(solution)/shard_map/all_to_all | solution.py:515
  78.4 5.7 %all-gather.3.cloned.1.call-done = bf16[16,2,512,128]{3,2,1,0:T(8,128)(2,1)} async-done(((bf16[2,2,512,128]{3,2,1,0:T(8,128)(2,1)}), bf16[16,2,512,128]{3,2,1,0:T(8,128)(2,1)}) %all-gather.3.cloned.1.call-update) | async-done | bytes 4194320 | tf_op jit(solution)/shard_map/all_gather | solution.py:536
  84.1 1.0 scan_prefix.1
  85.8 6.9 %all-to-all-start.1 = ((bf16[32,64,128]{2,1,0:T(8,128)(2,1)}), bf16[32,64,128]{2,1,0:T(8,128)(2,1)S(1)}, u32[]{:S(2)}, u32[]{:S(2)}) async-start(bf16[32,64,128]{2,1,0:T(8,128)(2,1)} %copy-done.4), calls=%async_computation.1 | async-start | bytes 1048576 | tf_op jit(solution)/shard_map/all_to_all | solution.py:515
  93.1 1.0 copy-done.2
  94.1 1.0 near_stats.1.near
  95.1 5.0 %far_stats.1 = f32[5,8,512]{2,1,0:T(8,128)S(1)} custom-call(s32[512]{0:T(512)S(1)} %reshape.29.codes, s32[1]{0:T(128)} %bitcast.me, f32[8,512]{1,0:T(8,128)S(1)} %near_stats.1.near, bf16[8,2,2,512,128]{4,3,2,1,0:T(8,128)(2,1)} %bitcast.50, bf16[4,2,2,512,128]{4,3,2,1,0:T(8,128)(2,1)S(1)} %pad_maximum_fusion.qos), custom_call_target="tpu_custom_call" | custom-call | flops 268435456 | bytes 6291456 | tf_op jit(solution)/shard_map/far_stats/pallas_call | solution.py:185
  100.0 2.9 %collective-permute-start.5 = (f32[5,8,512]{2,1,0:T(8,128)S(1)}, f32[5,8,512]{2,1,0:T(8,128)S(1)}, u32[]{:S(2)}, u32[]{:S(2)}) collective-permute-start(f32[5,8,512]{2,1,0:T(8,128)S(1)} %far_stats.1), channel_id=1, source_target_pairs={{0,192},{8,200},{16,208},{24,216},{32,224},{40,232},{48,240},{56,2... | collective-permute-start | bytes 245768 | tf_op jit(solution)/shard_map/ppermute | solution.py:522
  103.0 1.1 collective-permute-start.4
  105.3 3.1 %collective-permute-done.4 = f32[5,8,512]{2,1,0:T(8,128)S(1)} collective-permute-done((f32[5,8,512]{2,1,0:T(8,128)S(1)}, f32[5,8,512]{2,1,0:T(8,128)S(1)}, u32[]{:S(2)}, u32[]{:S(2)}) %collective-permute-start.4) | collective-permute-done | bytes 81952 | tf_op jit(solution)/shard_map/ppermute | solution.py:522
  108.4 2.6 %collective-permute-done.3 = f32[5,8,512]{2,1,0:T(8,128)S(1)} collective-permute-done((f32[5,8,512]{2,1,0:T(8,128)S(1)}, f32[5,8,512]{2,1,0:T(8,128)S(1)}, u32[]{:S(2)}, u32[]{:S(2)}) %collective-permute-start.3) | collective-permute-done | bytes 81952 | tf_op jit(solution)/shard_map/ppermute | solution.py:522
  111.0 12.6 %far_grads.1 = (bf16[8,2048,128]{2,1,0:T(8,128)(2,1)}, bf16[4,2,512,128]{3,2,1,0:T(8,128)(2,1)}) custom-call(s32[512]{0:T(512)S(1)} %reshape.29.codes, s32[1]{0:T(128)} %bitcast.me, f32[4,5,8,512]{3,2,1,0:T(8,128)S(1)} %pad_maximum_fusion.3.stats, bf16[8,2,2,512,128]{4,3,2,1,0:T(8,128)(2,1)} %bitcast.51, bf16[4,2,2,512,128]{4,3,2,1,0:T(8,128)(2,1)S(1)} %pad_maximum_fusion.qos), custom_call_target="tpu_custom_call" | custom-call | flops 671088640 | bytes 12582912 | tf_op jit(solution)/shard_map/far_grads/pallas_call | solution.py:266
  124.9 1.2 copy-done.10
  126.2 1.6 copy-done.16
  127.8 12.6 %scan_grads.1 = (bf16[512,1024]{1,0:T(8,128)(2,1)}, f32[512,16]{1,0:T(8,128)S(1)}, bf16[1024,128]{1,0:T(8,128)(2,1)S(1)}) custom-call(bf16[512,1024]{1,0:T(8,128)(2,1)S(1)} %copy-done.8, bf16[512,1024]{1,0:T(8,128)(2,1)S(1)} %copy-done.10, f32[512,16]{1,0:T(8,128)S(1)} %copy-done.6, bf16[512,128]{1,0:T(8,128)(2,1)S(1)} %copy-done.12, ...), custom_call_target="tpu_custom_call" | custom-call | flops 4294967296 | bytes 12582912 | tf_op jit(solution)/shard_map/scan_grads/pallas_call | solution.py:494
  140.4 11.7 %all_to_all.21 = bf16[8,128,128]{2,1,0:T(8,128)(2,1)S(1)} all-to-all(bf16[8,128,128]{2,1,0:T(8,128)(2,1)S(1)} %bitcast.49), channel_id=1, replica_groups=mesh['seq'=32,'head'=8] {'head'}, dimensions={0} | all-to-all | bytes 524288 | tf_op jit(solution)/shard_map/all_to_all | solution.py:553
  152.1 5.4 %all-to-all-start.2 = ((bf16[4,2,512,128]{3,2,1,0:T(8,128)(2,1)}), bf16[4,2,512,128]{3,2,1,0:T(8,128)(2,1)}, u32[]{:S(2)}, u32[]{:S(2)}) async-start(bf16[4,2,512,128]{3,2,1,0:T(8,128)(2,1)} %get-tuple-element.28), calls=%async_computation.2 | async-start | bytes 2097152 | tf_op jit(solution)/shard_map/all_to_all | solution.py:515
  158.3 14.0 %all_gather.11 = bf16[1024,128]{1,0:T(8,128)(2,1)S(1)} all-gather(bf16[128,128]{1,0:T(8,128)(2,1)S(1)} %reduce_sum.22), channel_id=1, replica_groups=mesh['seq'=32,'head'=8] {'head'}, dimensions={0}, use_global_device_ids=true | all-gather | bytes 294912 | tf_op jit(solution)/shard_map/all_gather | solution.py:555
  173.1 2.9 %near_grads.1 = (f32[2,512,128]{2,1,0:T(8,128)S(1)}, f32[2,2,512,128]{3,2,1,0:T(8,128)S(1)}) custom-call(s32[1]{0:T(128)} %bitcast.me, f32[4,5,8,512]{3,2,1,0:T(8,128)S(1)} %pad_maximum_fusion.3.stats, bf16[2,2,512,128]{3,2,1,0:T(8,128)(2,1)S(1)} %copy-done.3, bf16[2,2,512,128]{3,2,1,0:T(8,128)(2,1)S(1)} %copy-done), custom_call_target="tpu_custom_call" | custom-call | flops 671088640 | bytes 4194304 | tf_op jit(solution)/shard_map/near_grads/pallas_call | solution.py:302
  176.0 1.4 convert_reduce_fusion
  177.5 1.0 copy.59
  178.5 3.5 %reduce-scatter.2.cloned.1.call-done = bf16[1,2048,128]{2,1,0:T(8,128)(2,1)} async-done(((bf16[8,2048,128]{2,1,0:T(8,128)(2,1)}), bf16[1,2048,128]{2,1,0:T(8,128)(2,1)}) %reduce-scatter.2.cloned.1.call-update) | async-done | bytes 524304 | tf_op jit(solution)/shard_map/reduce_scatter | solution.py:547
  182.0 1.1 fusion
  183.2 1.0 copy.61
  184.1 1.0 copy.60
  (78 shorter events, 9.9 us)
Async XLA Ops:
  7.2 76.9 %all-gather.3.cloned.1.call-start = ((), (), s32[]{:S(2)}) async-start(), calls=%async_computation.6 | async-start | bytes 4718592 | tf_op jit(solution)/shard_map/all_gather | solution.py:536
  10.2 1.1 copy-start.18
  10.3 1.4 copy-start.19
  11.7 5.9 %copy-start.20 = (f32[512,16]{0,1:T(8,128)S(1)}, f32[512,16]{0,1:T(8,128)}, u32[]{:S(2)}) copy-start(f32[512,16]{0,1:T(8,128)} %param.17) | copy-start | bytes 98308
  12.1 5.6 %copy-start.7 = (bf16[512,1024]{1,0:T(8,128)(2,1)S(1)}, bf16[512,1024]{1,0:T(8,128)(2,1)}, u32[]{:S(2)}) copy-start(bf16[512,1024]{1,0:T(8,128)(2,1)} %x_ref.3) | copy-start | bytes 3145732
  12.1 5.6 %copy-start.9 = (bf16[512,1024]{1,0:T(8,128)(2,1)S(1)}, bf16[512,1024]{1,0:T(8,128)(2,1)}, u32[]{:S(2)}) copy-start(bf16[512,1024]{1,0:T(8,128)(2,1)} %g_ref.3) | copy-start | bytes 3145732
  12.1 5.6 %copy-start.11 = (bf16[512,128]{1,0:T(8,128)(2,1)S(1)}, bf16[512,128]{1,0:T(8,128)(2,1)}, u32[]{:S(2)}) copy-start(bf16[512,128]{1,0:T(8,128)(2,1)} %b_ref.3) | copy-start | bytes 393220
  12.1 5.6 %copy-start.13 = (bf16[512,128]{1,0:T(8,128)(2,1)S(1)}, bf16[512,128]{1,0:T(8,128)(2,1)}, u32[]{:S(2)}) copy-start(bf16[512,128]{1,0:T(8,128)(2,1)} %c_ref.3) | copy-start | bytes 393220
  13.1 9.0 %copy-start.1 = (bf16[2,2,512,128]{3,2,1,0:T(8,128)(2,1)}, bf16[2,2,512,128]{3,2,1,0:T(8,128)(2,1)S(1)}, u32[]{:S(2)}) copy-start(bf16[2,2,512,128]{3,2,1,0:T(8,128)(2,1)S(1)} %get-tuple-element.63.qo) | copy-start | bytes 1572868
  13.1 17.0 %collective-permute-start.2 = (bf16[2,2,512,128]{3,2,1,0:T(8,128)(2,1)S(1)}, bf16[2,2,512,128]{3,2,1,0:T(8,128)(2,1)}, u32[]{:S(2)}, u32[]{:S(2)}) collective-permute-start(bf16[2,2,512,128]{3,2,1,0:T(8,128)(2,1)S(1)} %get-tuple-element.63.qo), channel_id=1, source_target_pairs={{0,192},{8,200},{16,208},{24,216},{32,224},{40,232},{48,240},{56,2... | collective-permute-start | bytes 1572872 | tf_op jit(solution)/shard_map/ppermute | solution.py:522
  16.4 14.1 %collective-permute-start.1 = (bf16[2,2,512,128]{3,2,1,0:T(8,128)(2,1)S(1)}, bf16[2,2,512,128]{3,2,1,0:T(8,128)(2,1)}, u32[]{:S(2)}, u32[]{:S(2)}) collective-permute-start(bf16[2,2,512,128]{3,2,1,0:T(8,128)(2,1)S(1)} %get-tuple-element.63.qo), channel_id=1, source_target_pairs={{0,128},{8,136},{16,144},{24,152},{32,160},{40,168},{48,176},{56,1... | collective-permute-start | bytes 1572872 | tf_op jit(solution)/shard_map/ppermute | solution.py:522
  17.0 26.2 %collective-permute-start = (bf16[2,2,512,128]{3,2,1,0:T(8,128)(2,1)S(1)}, bf16[2,2,512,128]{3,2,1,0:T(8,128)(2,1)}, u32[]{:S(2)}, u32[]{:S(2)}) collective-permute-start(bf16[2,2,512,128]{3,2,1,0:T(8,128)(2,1)S(1)} %get-tuple-element.63.qo), channel_id=1, source_target_pairs={{0,64},{8,72},{16,80},{24,88},{32,96},{40,104},{48,112},{56,120},{... | collective-permute-start | bytes 1572872 | tf_op jit(solution)/shard_map/ppermute | solution.py:522
  17.7 25.4 %copy-start.5 = (f32[512,16]{1,0:T(8,128)}, f32[512,16]{1,0:T(8,128)S(1)}, u32[]{:S(2)}) copy-start(f32[512,16]{1,0:T(8,128)S(1)} %copy.57.ld_ref) | copy-start | bytes 98308
  17.8 25.4 %copy-start.17 = (bf16[1,2,2,512,128]{4,3,2,1,0:T(8,128)(2,1)S(1)}, bf16[1,2,2,512,128]{4,3,2,1,0:T(8,128)(2,1)}, u32[]{:S(2)}) copy-start(bf16[1,2,2,512,128]{4,3,2,1,0:T(8,128)(2,1)} %get-tuple-element.62) | copy-start | bytes 1572868
  22.2 22.6 %copy-start.15 = (f32[4,1024,128]{2,1,0:T(8,128)}, f32[4,1024,128]{2,1,0:T(8,128)S(1)}, u32[]{:S(2)}) copy-start(f32[4,1024,128]{2,1,0:T(8,128)S(1)} %get-tuple-element.33.ends) | copy-start | bytes 6291460
  44.8 48.0 %copy-start.21 = (s32[128,4]{0,1:T(4,128)S(1)}, s32[128,4]{0,1:T(4,128)}, u32[]{:S(2)}) copy-start(s32[128,4]{0,1:T(4,128)} %param.22) | copy-start | bytes 6148
  44.8 48.0 %copy-start.22 = (s32[128,4]{0,1:T(4,128)S(1)}, s32[128,4]{0,1:T(4,128)}, u32[]{:S(2)}) copy-start(s32[128,4]{0,1:T(4,128)} %param.21) | copy-start | bytes 6148
  44.8 48.0 %copy-start.23 = (s32[128]{0:T(128)S(1)}, s32[128]{0:T(128)}, u32[]{:S(2)}) copy-start(s32[128]{0:T(128)} %param.23) | copy-start | bytes 1540
  44.8 48.2 %copy-start = (bf16[2,2,512,128]{3,2,1,0:T(8,128)(2,1)S(1)}, bf16[2,2,512,128]{3,2,1,0:T(8,128)(2,1)}, u32[]{:S(2)}) copy-start(bf16[2,2,512,128]{3,2,1,0:T(8,128)(2,1)} %pad_maximum_fusion.2.kv) | copy-start | bytes 1572868
  85.8 25.1 %all-to-all-start.1 = ((bf16[32,64,128]{2,1,0:T(8,128)(2,1)}), bf16[32,64,128]{2,1,0:T(8,128)(2,1)S(1)}, u32[]{:S(2)}, u32[]{:S(2)}) async-start(bf16[32,64,128]{2,1,0:T(8,128)(2,1)} %copy-done.4), calls=%async_computation.1 | async-start | bytes 1048576 | tf_op jit(solution)/shard_map/all_to_all | solution.py:515
  92.7 89.2 %reduce-scatter.2.cloned.1.call-start = ((), (), s32[]{:S(2)}) async-start(), calls=%async_computation.5 | async-start | bytes 4718592 | tf_op jit(solution)/shard_map/reduce_scatter | solution.py:547
  93.0 1.0 copy-start.2
  100.0 5.3 %collective-permute-start.5 = (f32[5,8,512]{2,1,0:T(8,128)S(1)}, f32[5,8,512]{2,1,0:T(8,128)S(1)}, u32[]{:S(2)}, u32[]{:S(2)}) collective-permute-start(f32[5,8,512]{2,1,0:T(8,128)S(1)} %far_stats.1), channel_id=1, source_target_pairs={{0,192},{8,200},{16,208},{24,216},{32,224},{40,232},{48,240},{56,2... | collective-permute-start | bytes 245768 | tf_op jit(solution)/shard_map/ppermute | solution.py:522
  103.0 5.4 %collective-permute-start.4 = (f32[5,8,512]{2,1,0:T(8,128)S(1)}, f32[5,8,512]{2,1,0:T(8,128)S(1)}, u32[]{:S(2)}, u32[]{:S(2)}) collective-permute-start(f32[5,8,512]{2,1,0:T(8,128)S(1)} %far_stats.1), channel_id=1, source_target_pairs={{0,128},{8,136},{16,144},{24,152},{32,160},{40,168},{48,176},{56,1... | collective-permute-start | bytes 245768 | tf_op jit(solution)/shard_map/ppermute | solution.py:522
  104.0 6.9 %collective-permute-start.3 = (f32[5,8,512]{2,1,0:T(8,128)S(1)}, f32[5,8,512]{2,1,0:T(8,128)S(1)}, u32[]{:S(2)}, u32[]{:S(2)}) collective-permute-start(f32[5,8,512]{2,1,0:T(8,128)S(1)} %far_stats.1), channel_id=1, source_target_pairs={{0,64},{8,72},{16,80},{24,88},{32,96},{40,104},{48,112},{56,120},{... | collective-permute-start | bytes 245768 | tf_op jit(solution)/shard_map/ppermute | solution.py:522
  123.6 1.3 copy-start.8
  123.6 1.3 copy-start.12
  123.6 1.3 copy-start.14
  124.9 1.2 copy-start.10
  126.2 1.6 copy-start.16
  152.1 21.0 %copy-start.3 = (bf16[2,2,512,128]{3,2,1,0:T(8,128)(2,1)S(1)}, bf16[2,2,512,128]{3,2,1,0:T(8,128)(2,1)}, u32[]{:S(2)}) copy-start(bf16[2,2,512,128]{3,2,1,0:T(8,128)(2,1)} %copy-done.1) | copy-start | bytes 1572868
  152.1 21.0 %all-to-all-start.2 = ((bf16[4,2,512,128]{3,2,1,0:T(8,128)(2,1)}), bf16[4,2,512,128]{3,2,1,0:T(8,128)(2,1)}, u32[]{:S(2)}, u32[]{:S(2)}) async-start(bf16[4,2,512,128]{3,2,1,0:T(8,128)(2,1)} %get-tuple-element.28), calls=%async_computation.2 | async-start | bytes 2097152 | tf_op jit(solution)/shard_map/all_to_all | solution.py:515
  (2 other events, 1.8 us)
Sparse Core Ops, SparseCore 0:
  11.4 72.6 all-gather.2
  123.8 58.1 reduce-scatter.1
where the time goes:
time: 192 us
  blocking collectives  59.3 us (31%)
  Pallas kernels  39.4 us (21%)
  waiting for transfers between devices  36.3 us (19%)
  starting transfers between devices  21.5 us (11%)
  local copies, waits for them, and re-layouts  14.7 us (8%)
  between operations  14.5 us (8%)
  other arithmetic  6.18 us (3%)
    all_to_all x1, blocking collectives, exchange(): lax.all_to_all(value, 'seq', 0, 0, tiled=True, axis_index_groups=groups)  33.5 us
    ppermute x6, waiting for transfers between devices, along_x(): return lax.ppermute(value, 'seq', pairs)  27.1 us
    all_gather x1, blocking collectives, per_device(): whole = lax.all_gather(part, 'head', tiled=True).astype(F32)  14 us
    pallas_call x1, Pallas kernels, far_grads(): call(far_grads_body, 'far_grads', [((NZ, 4 * TOK, HD), BF16, vm), ((NX, 2...  12.6 us
    pallas_call x1, Pallas kernels, scan_grads(): call(grads_body, 'scan_grads', [((TOK, WIDTH), BF16, vm), ((TOK, SH), F32...  12.6 us
    all_to_all x2, starting transfers between devices, exchange(): lax.all_to_all(value, 'seq', 0, 0, tiled=True, axis_index_groups=groups)  12.3 us
    all_to_all x1, blocking collectives, per_device(): shares = lax.all_to_all(bc.reshape(8, 128, NST), 'head', 0, 0, tiled=True)  11.7 us
    unnamed x53, local copies, waits for them, and re-layouts  9.79 us
  transfers between devices with their start and end apart: 10, of which 8 were waited for; matrix products, arithmetic and copies ran while one was open for 4% of the time, Pallas kernels for 13%

commit v1 on v0

--- a/solution.py
+++ b/solution.py
@@ -68,49 +68,48 @@
 EMPTY = -1e30
 KINDS = 3
 FAR = NZ * SEG
-
-
-def list_items(codes, me, places, blocks):
-    here = me[0]
-    my_x = here >> 3
-    my_z = here & (NZ - 1)
-    count = jnp.int32(0)
-    for d in range(NX):
-        base = (((my_x - d) & (NX - 1)) * NZ + my_z) * ITEMS
-
-        def item(i, n, d=d, base=base):
-            code = codes[base + i]
-            places[n] = code & (FAR - 1)
-            blocks[n] = d * SEG + (i >> 2)
-            return n + ((code >= 0) & ((code >> 5) == my_x)).astype(jnp.int32)
-
-        count = lax.fori_loop(0, ITEMS, item, count)
-    places[count] = 0
-    blocks[count] = NX * SEG
-    return count
+UNROLL = 4
+PAIR = 2 * HD
+
+
+def far_items(codes, me):
+    my_x = me[0] >> 3
+    my_z = me[0] & (NZ - 1)
+    sources = ((my_x - jnp.arange(NX)) & (NX - 1)) * NZ + my_z
+    code = jnp.take(codes.reshape(NS, ITEMS), sources, axis=0).reshape(NX * ITEMS)
+    block = jnp.arange(NX * ITEMS) // GLOB
+    hit = (code >= 0) & ((code >> 5) == my_x)
+    order = jnp.arange(NX * ITEMS)
+    rank = jnp.sum((hit[None, :] & (order[None, :] < order[:, None])).astype(jnp.int32), axis=1)
+    slot = jnp.arange(NX * ITEMS + UNROLL)[:, None]
+    chosen = hit[None, :] & (rank[None, :] == slot)
+    places = jnp.sum(jnp.where(chosen, code[None, :] & (FAR - 1), 0), axis=1)
+    blocks = NX * SEG + jnp.sum(jnp.where(chosen, block[None, :] - NX * SEG, 0), axis=1)
+    count = jnp.sum(hit.astype(jnp.int32)).reshape(1)
+    return jnp.concatenate([count, places, blocks]).astype(jnp.int32)
+
+
+class Listed:
+    def __init__(self, ref):
+        self.count = ref[0]
+        self.place = lambda n: ref[1 + n]
+        self.block = lambda n: ref[1 + NX * ITEMS + UNROLL + n]
 
 
 def span(index):
     return pl.ds(pl.multiple_of(index * BLK, BLK), BLK)
 
 
-def pairs(count, visit):
-    def two(t, _):
-        visit([2 * t, 2 * t + 1])
+def in_groups(count, visit):
+    def group(t, _):
+        visit([UNROLL * t + i for i in range(UNROLL)])
         return 0
 
-    lax.fori_loop(0, (count + 1) >> 1, two, 0)
-
-
-def fetch(qos, keys, place, block):
-    d = jnp.minimum(block >> 2, NX - 1)
-    rows = span(block & (SEG - 1))
-    z = place >> 2
-    cols = span(place & (SEG - 1))
-    return [
-        (qos[d, h, 0, rows, :], qos[d, h, 1, rows, :], keys[z, h, 0, cols, :], keys[z, h, 1, cols, :])
-        for h in range(2)
-    ]
+    lax.fori_loop(0, (count + UNROLL - 1) // UNROLL, group, 0)
+
+
+def head(h):
+    return pl.ds(h * HD, HD)
 
 
 def summary(q, o, k, v):
@@ -118,20 +117,36 @@
     dp = mm_nt(v, o)
     m = jnp.max(s, axis=0, keepdims=True)
     e = jnp.exp(s - m)
-    return m, jnp.sum(e, axis=0, keepdims=True), jnp.sum(e * dp, axis=0, keepdims=True)
-
-
-def stack_rows(rows):
-    return jnp.concatenate(rows + [jnp.zeros((8 - len(rows), rows[0].shape[1]), F32)], axis=0)
+    return [m, jnp.sum(e, axis=0, keepdims=True), jnp.sum(e * dp, axis=0, keepdims=True)]
+
+
+def packed(quads):
+    return jnp.concatenate(
+        [jnp.concatenate([quads[i], quads[i + 2]], axis=0) for i in range(2)], axis=1
+    )
+
+
+def unpacked(tile, b):
+    at = 4 * (b >> 1)
+    return tile[at : at + KINDS, (b & 1) * PAIR : (b & 1) * PAIR + PAIR]
 
 
 def near_stats_body(qo, kv, out):
+    quads = []
     for b in range(SEG):
         rows = pl.ds(b * BLK, BLK)
-        parts = []
-        for h in range(2):
-            parts += summary(qo[h, 0, rows, :], qo[h, 1, rows, :], kv[h, 0], kv[h, 1])
-        out[:, rows] = stack_rows(parts)
+        heads = [
+            summary(qo[0, rows, head(h)], qo[1, rows, head(h)], kv[0, :, head(h)], kv[1, :, head(h)])
+            for h in range(2)
+        ]
+        quads.append(
+            jnp.concatenate(
+                [jnp.concatenate([x, y], axis=1) for x, y in zip(*heads)]
+                + [jnp.zeros((1, PAIR), F32)],
+                axis=0,
+            )
+        )
+    out[...] = packed(quads)
 
 
 def near_stats(qo, kv):
@@ -139,7 +154,7 @@
     return call(
         near_stats_body,
         "near_stats",
-        [((8, TOK), F32, vm)],
+        [((8, 2 * PAIR), F32, vm)],
         [vm, vm],
         [],
         2 * 2 * 2 * TOK * TOK * HD,
@@ -147,50 +162,91 @@
     )(qo, kv)[0]
 
 
-def far_stats_body(codes, me, near, column, qos, out, tally, places, blocks):
-    count = list_items(codes, me, places, blocks)
-    kind = lax.broadcasted_iota(jnp.int32, (8, BLK), 0)
-    start = jnp.where((kind == 0) | (kind == KINDS), EMPTY, 0.0)
+def spread(value):
+    lane = lax.broadcasted_iota(jnp.int32, (BLK, PAIR), 1)
+    zero = jnp.zeros((BLK, PAIR), BF16)
+    return jnp.concatenate(
+        [jnp.where(lane < HD, value, zero), jnp.where(lane < HD, zero, value)], axis=0
+    )
+
+
+def load(pieces, sems):
+    copies = [pltpu.make_async_copy(a, b, sems.at[i]) for i, (a, b) in enumerate(pieces)]
+    for copy in copies:
+        copy.start()
+
+    def wait():
+        for copy in copies:
+            copy.wait()
+
+    return wait
+
+
+def load_far(column_in, qos_in, column, qos, sems):
+    return load(
+        [(column_in.at[z], column.at[z]) for z in range(NZ)]
+        + [(qos_in.at[d], qos.at[d]) for d in range(NX)],
+        sems,
+    )
+
+
+def far_scratch():
+    return [
+        pltpu.VMEM((NZ, 2, TOK, PAIR), BF16),
+        pltpu.VMEM((NX, 2, TOK, PAIR), BF16),
+        pltpu.SemaphoreType.DMA((NZ + NX,)),
+    ]
+
+
+def fetch(qos, keys, place, block):
+    n = jnp.minimum(block, NX * SEG - 1)
+    d = n >> 2
+    rows = span(n & (SEG - 1))
+    z = place >> 2
+    cols = span(place & (SEG - 1))
+    return (
+        spread(qos[d, 0, rows, :]), spread(qos[d, 1, rows, :]), keys[z, 0, cols, :], keys[z, 1, cols, :]
+    )
+
+
+def far_stats_body(listed, near, column_in, qos_in, out, tally, column, qos, sems):
+    ready = load_far(column_in, qos_in, column, qos, sems)
+    items = Listed(listed)
+    kind = lax.broadcasted_iota(jnp.int32, (4, PAIR), 0)
+    start = jnp.where(kind == 0, EMPTY, 0.0)
     for n in range(NX * SEG + 1):
         tally[n] = start
-
-    def visit(items):
-        found = []
-        for n in items:
-            found.append([summary(*part) for part in fetch(qos, column, places[n], blocks[n])])
-        for n, heads in zip(items, found):
-            old = tally[blocks[n]]
-            rows = []
-            for h, (m, l, t) in enumerate(heads):
-                m0, l0, t0 = [old[KINDS * h + i : KINDS * h + i + 1, :] for i in range(KINDS)]
-                high = jnp.maximum(m0, m)
-                f0 = jnp.exp(m0 - high)
-                f1 = jnp.exp(m - high)
-                rows += [high, l0 * f0 + l * f1, t0 * f0 + t * f1]
-            tally[blocks[n]] = stack_rows(rows)
-
-    pairs(count, visit)
+    ready()
+
+    def visit(numbers):
+        found = [summary(*fetch(qos, column, items.place(n), items.block(n))) for n in numbers]
+        for n, (m, l, t) in zip(numbers, found):
+            old = tally[items.block(n)]
+            m0, l0, t0 = [old[i : i + 1, :] for i in range(KINDS)]
+            high = jnp.maximum(m0, m)
+            f0 = jnp.exp(m0 - high)
+            f1 = jnp.exp(m - high)
+            tally[items.block(n)] = jnp.concatenate(
+                [high, l0 * f0 + l * f1, t0 * f0 + t * f1, jnp.zeros_like(high)], axis=0
+            )
+
+    in_groups(items.count, visit)
     for d in range(NX):
-        for b in range(SEG):
-            out[d, :, pl.ds(b * BLK, BLK)] = tally[d * SEG + b]
+        out[d] = packed([tally[d * SEG + b] for b in range(SEG)])
     out[NX] = near[...]
 
 
-def item_scratch():
-    return [pltpu.SMEM((NX * ITEMS + 1,), jnp.int32)] * 2
-
-
-def far_stats(codes, me, near, column, qos):
+def far_stats(listed, near, column, qos):
     vm = pltpu.VMEM
     return call(
         far_stats_body,
         "far_stats",
-        [((NX + 1, 8, TOK), F32, vm)],
-        [pltpu.SMEM, pltpu.SMEM] + [vm] * 3,
-        [vm((NX * SEG + 1, 8, BLK), F32)] + item_scratch(),
+        [((NX + 1, 8, 2 * PAIR), F32, vm)],
+        [pltpu.SMEM, vm, pltpu.HBM, pl.ANY],
+        [vm((NX * SEG + 1, 4, PAIR), F32)] + far_scratch(),
         2 * 2 * 2 * 16 * BLK * BLK * HD,
         6 << 20,
-    )(codes, me, near, column, qos)[0]
+    )(listed, near, column, qos)[0]
 
 
 def joined(stats, my_x, x_q):
@@ -200,15 +256,14 @@
         parts.append(stats[r, (x - x_q) & (NX - 1)])
     parts.append(stats[(my_x - x_q) & (NX - 1), NX])
     rows = []
-    for h in range(2):
-        at = KINDS * h
+    for at in (0, 4):
         high = functools.reduce(jnp.maximum, [p[at : at + 1, :] for p in parts])
         fade = [jnp.exp(p[at : at + 1, :] - high) for p in parts]
         total = sum(f * p[at + 1 : at + 2, :] for f, p in zip(fade, parts))
         mixed = sum(f * p[at + 2 : at + 3, :] for f, p in zip(fade, parts))
         inverse = 1.0 / total
-        rows += [high, inverse, mixed * inverse]
-    return stack_rows(rows)
+        rows += [high, inverse, mixed * inverse, jnp.zeros_like(high)]
+    return jnp.concatenate(rows, axis=0)
 
 
 def weights_of(q, o, k, v, row):
@@ -218,96 +273,227 @@
     return p.astype(BF16), ds
 
 
+def ds_copies(a, b, sems):
+    def group(t):
+        tiles = pl.ds(UNROLL * t, UNROLL)
+        return pltpu.make_async_copy(a.at[tiles], b.at[tiles], sems.at[t])
+
+    return group
+
+
 def far_grads_body(
-    codes, me, stats, column, qos, kv_out, dq_out, total, dq, rowed, places, blocks
+    listed, me, stats, column_in, qos_in, kv_out, ds_out,
+    total, rowed, staged, ds_keep, column, qos, sems, out_sems, ds_sems,
 ):
+    ready = load_far(column_in, qos_in, column, qos, sems)
     my_x = me[0] >> 3
-    count = list_items(codes, me, places, blocks)
+    items = Listed(listed)
+    sent = ds_copies(ds_keep, ds_out, ds_sems)
     total[...] = jnp.zeros_like(total)
+    for d in range(NX):
+        tile = joined(stats, my_x, (my_x - d) & (NX - 1))
+        for b in range(SEG):
+            rowed[d * SEG + b, 0:KINDS, :] = unpacked(tile, b)
+    rowed[NX * SEG] = jnp.zeros((8, PAIR), F32)
+    ready()
+
+    def group(t, _):
+        numbers = [UNROLL * t + i for i in range(UNROLL)]
+        found = []
+        for n in numbers:
+            q, o, k, v = fetch(qos, column, items.place(n), items.block(n))
+            p, ds = weights_of(q, o, k, v, rowed[items.block(n)])
+            found.append((ds, mm(ds, q), mm(p, o)))
+        for n, (ds, dk, dv) in zip(numbers, found):
+            to = jnp.where(items.block(n) == NX * SEG, FAR, items.place(n))
+            ds_keep[n] = ds
+            total[to, 0] += dk
+            total[to, 1] += dv
+        sent(t).start()
+        return 0
+
+    groups = (items.count + UNROLL - 1) // UNROLL
+    lax.fori_loop(0, groups, group, 0)
+    copies = []
+    for z in range(NZ):
+        for s in range(2):
+            for b in range(SEG):
+                staged[z, pl.ds(s * TOK + b * BLK, BLK), :] = total[z * SEG + b, s].astype(BF16)
+        copies.append(pltpu.make_async_copy(staged.at[z], kv_out.at[z], out_sems.at[z]))
+        copies[-1].start()
+
+    def drain(t, _):
+        sent(t).wait()
+        return 0
+
+    lax.fori_loop(0, groups, drain, 0)
+    for copy in copies:
+        copy.wait()
+
+
+def far_grads(listed, me, stats, column, qos):
+    vm = pltpu.VMEM
+    tiles = NX * ITEMS + UNROLL
+    return call(
+        far_grads_body,
+        "far_grads",
+        [
+            ((NZ, 2 * TOK, PAIR), BF16, pltpu.HBM),
+            ((tiles, BLK, PAIR), BF16, pltpu.HBM),
+        ],
+        [pltpu.SMEM, pltpu.SMEM, vm, pltpu.HBM, pl.ANY],
+        [
+            vm((FAR + 1, 2, BLK, PAIR), F32),
+            vm((NX * SEG + 1, 8, PAIR), F32),
+            vm((NZ, 2 * TOK, PAIR), BF16),
+            vm((tiles, BLK, PAIR), BF16),
+        ]
+        + far_scratch()
+        + [pltpu.SemaphoreType.DMA((NZ,)), pltpu.SemaphoreType.DMA((tiles // UNROLL,))],
+        4 * 2 * 2 * 16 * BLK * BLK * HD,
+        12 << 20,
+    )(listed, me, stats, column, qos)
+
+
+def far_queries_body(listed, me, ds_in, column_in, dq_out, dq, ds_keep, keys, sems, ds_sems):
+    ready = load([(column_in.at[z, 0], keys.at[z]) for z in range(NZ)], sems)
+    my_x = me[0] >> 3
+    items = Listed(listed)
+    fetched = ds_copies(ds_in, ds_keep, ds_sems)
+    groups = (items.count + UNROLL - 1) // UNROLL
+
+    def begin(t, _):
+        fetched(t).start()
+        return 0
+
+    lax.fori_loop(0, groups, begin, 0)
     dq[...] = jnp.zeros_like(dq)
-    for d in range(NX):
-        row = joined(stats, my_x, (my_x - d) & (NX - 1))
-        for b in range(SEG):
-            rowed[d * SEG + b] = row[:, b * BLK : (b + 1) * BLK]
-    rowed[NX * SEG] = jnp.zeros((8, BLK), F32)
-
-    def visit(items):
+    ready()
+
+    def group(t, _):
+        fetched(t).wait()
+        numbers = [UNROLL * t + i for i in range(UNROLL)]
         found = []
-        for n in items:
-            row = rowed[blocks[n]]
-            heads = fetch(qos, column, places[n], blocks[n])
-            grads = []
-            for h, (q, o, k, v) in enumerate(heads):
-                p, ds = weights_of(q, o, k, v, row[KINDS * h : KINDS * h + KINDS, :])
-                grads.append((mm_tn(ds, k), mm(ds, q), mm(p, o)))
-            found.append(grads)
-        for n, grads in zip(items, found):
-            at = blocks[n]
-            to = jnp.where(at == NX * SEG, FAR, places[n])
-            for h, (dqh, dkh, dvh) in enumerate(grads):
-                dq[at, h] += dqh
-                total[to, h, 0] += dkh
-                total[to, h, 1] += dvh
-
-    pairs(count, visit)
+        for n in numbers:
+            place = items.place(n)
+            k = keys[place >> 2, span(place & (SEG - 1)), :]
+            ds = ds_keep[n]
+            found.append(
+                [mm_tn(ds[:, h * HD : h * HD + HD], k[:, h * HD : h * HD + HD]) for h in range(2)]
+            )
+        for n, heads in zip(numbers, found):
+            for h in range(2):
+                dq[items.block(n), :, head(h)] += heads[h]
+        return 0
+
+    lax.fori_loop(0, groups, group, 0)
     for d in range(NX):
         for b in range(SEG):
-            dq_out[(my_x - d) & (NX - 1), :, pl.ds(b * BLK, BLK), :] = dq[d * SEG + b].astype(BF16)
-    for z in range(NZ):
-        for h in range(2):
-            for s in range(2):
-                for b in range(SEG):
-                    at = (2 * h + s) * TOK + b * BLK
-                    kv_out[z, pl.ds(at, BLK), :] = total[z * SEG + b, h, s].astype(BF16)
-
-
-def far_grads(codes, me, stats, column, qos):
-    vm = pltpu.VMEM
-    return call(
-        far_grads_body,
-        "far_grads",
-        [((NZ, 4 * TOK, HD), BF16, vm), ((NX, 2, TOK, HD), BF16, vm)],
-        [pltpu.SMEM, pltpu.SMEM] + [vm] * 3,
+            dq_out[(my_x - d) & (NX - 1), pl.ds(b * BLK, BLK), :] = dq[d * SEG + b].astype(BF16)
+
+
+def far_queries(listed, me, ds, column):
+    vm = pltpu.VMEM
+    tiles = NX * ITEMS + UNROLL
+    return call(
+        far_queries_body,
+        "far_queries",
+        [((NX, TOK, PAIR), BF16, vm)],
+        [pltpu.SMEM, pltpu.SMEM, pltpu.HBM, pltpu.HBM],
         [
-            vm((FAR + 1, 2, 2, BLK, HD), F32),
-            vm((NX * SEG + 1, 2, BLK, HD), F32),
-            vm((NX * SEG + 1, 8, BLK), F32),
-        ]
-        + item_scratch(),
-        5 * 2 * 2 * 16 * BLK * BLK * HD,
-        12 << 20,
-    )(codes, me, stats, column, qos)
-
-
-def near_grads_body(me, stats, qo, kv, dq_out, kv_out, p_keep, s_keep):
+            vm((NX * SEG + 1, BLK, PAIR), F32),
+            vm((tiles, BLK, PAIR), BF16),
+            vm((NZ, TOK, PAIR), BF16),
+            pltpu.SemaphoreType.DMA((NZ,)),
+            pltpu.SemaphoreType.DMA((tiles // UNROLL,)),
+        ],
+        2 * 2 * 16 * BLK * BLK * HD,
+        6 << 20,
+    )(listed, me, ds, column)[0]
+
+
+def interleave(out, rows, value):
+    for h in range(2):
+        rows[pl.ds(h, TOK, stride=2), :] = value[:, h * HD : h * HD + HD]
+    out[...] = rows[...].astype(BF16)
+
+
+def near_grads_body(me, stats, qo, kv, dq_far, dq_out, kv_out, p_keep, s_keep, dq, rows_keep):
     my_x = me[0] >> 3
-    row = joined(stats, my_x, my_x)
+    tile = joined(stats, my_x, my_x)
     for h in range(2):
-        k = kv[h, 0]
+        k = kv[0, :, head(h)]
         for b in range(SEG):
             rows = pl.ds(b * BLK, BLK)
             p, ds = weights_of(
-                qo[h, 0, rows, :], qo[h, 1, rows, :], k, kv[h, 1],
-                row[KINDS * h : KINDS * h + KINDS, b * BLK : (b + 1) * BLK],
+                qo[0, rows, head(h)], qo[1, rows, head(h)], k, kv[1, :, head(h)],
+                unpacked(tile, b)[:, h * HD : h * HD + HD],
             )
-            dq_out[h, rows, :] = mm_tn(ds, k)
+            part = mm_tn(ds, k)
+            for x in range(NX):
+                part = part + dq_far[x, rows, head(h)].astype(F32)
+            dq[rows, head(h)] = part
             p_keep[:, rows] = p
             s_keep[:, rows] = ds
-        kv_out[h, 0] = mm(s_keep[...], qo[h, 0])
-        kv_out[h, 1] = mm(p_keep[...], qo[h, 1])
-
-
-def near_grads(me, stats, qo, kv):
+        kv_out[0, :, head(h)] = mm(s_keep[...], qo[0, :, head(h)])
+        kv_out[1, :, head(h)] = mm(p_keep[...], qo[1, :, head(h)])
+    interleave(dq_out, rows_keep, dq[...])
+
+
+def near_grads(me, stats, qo, kv, dq_far):
     vm = pltpu.VMEM
     return call(
         near_grads_body,
         "near_grads",
-        [((2, TOK, HD), F32, vm), ((2, 2, TOK, HD), F32, vm)],
-        [pltpu.SMEM] + [vm] * 3,
-        [vm((TOK, TOK), BF16), vm((TOK, TOK), BF16)],
+        [((2 * TOK, HD), BF16, vm), ((2, TOK, PAIR), F32, vm)],
+        [pltpu.SMEM] + [vm] * 4,
+        [
+            vm((TOK, TOK), BF16),
+            vm((TOK, TOK), BF16),
+            vm((TOK, PAIR), F32),
+            vm((2 * TOK, HD), F32),
+        ],
         5 * 2 * 2 * TOK * TOK * HD,
         4 << 20,
-    )(me, stats, qo, kv)
+    )(me, stats, qo, kv, dq_far)
+
+
+def finish_body(near, far, dk, dv, rows):
+    for s, out in enumerate((dk, dv)):
+        interleave(out, rows, near[s] + far[pl.ds(s * TOK, TOK), :].astype(F32))
+
+
+def finish(near, far):
+    vm = pltpu.VMEM
+    return call(
+        finish_body,
+        "finish",
+        [((2 * TOK, HD), BF16, vm)] * 2,
+        [vm] * 2,
+        [vm((2 * TOK, HD), F32)],
+        0,
+        2 << 20,
+    )(near, far)
+
+
+def by_head_body(first, second, out, rows):
+    for s, ref in enumerate((first, second)):
+        rows[...] = ref[...].astype(F32)
+        for h in range(2):
+            out[s, :, head(h)] = rows[pl.ds(h, TOK, stride=2), :].astype(BF16)
+
+
+def by_head(first, second):
+    vm = pltpu.VMEM
+    return call(
+        by_head_body,
+        "by_head",
+        [((2, TOK, PAIR), BF16, vm)],
+        [vm] * 2,
+        [vm((2 * TOK, HD), F32)],
+        0,
+        1 << 20,
+    )(first.reshape(2 * TOK, HD), second.reshape(2 * TOK, HD))[0]
 
 
 def triangle(lower):
@@ -528,38 +714,39 @@
 
 def per_device(q, k, v, o, x, ld, b, c, g, owner, offset, count):
     me = lax.axis_index("seq").astype(jnp.int32).reshape(1)
+    kv = by_head(k, v)
+    column = lax.all_gather(kv, "seq", axis_index_groups=Z_GROUPS)
+    qo = by_head(q, o)
     live = jnp.arange(GLOB)[None, :] < count[:, None]
     codes = jnp.where(live, owner * SEG + offset, -1).reshape(NS * ITEMS)
-    heads = range(q.shape[1])
-    kv = jnp.stack([jnp.stack([k[:, h], v[:, h]]) for h in heads])
-    qo = jnp.stack([jnp.stack([q[:, h], o[:, h]]) for h in heads])
-    column = lax.all_gather(kv, "seq", axis_index_groups=Z_GROUPS)
-    qos = jnp.stack([qo] + [along_x(qo, d) for d in range(1, NX)])
+    listed = far_items(codes, me)
+    shifted = [along_x(qo, 1), along_x(qo, 3)]
+    opposite = jnp.concatenate([along_x(shifted[0][:1], 1), along_x(shifted[1][1:], 3)])
+    qos = jnp.stack([qo, shifted[0], opposite, shifted[1]])
     near = near_stats(qo, kv)
     ends, starts, pay = scan_ends(x, g, ld, b, c)
-    pay = exchange(after(pay, qos))
-    carried = exchange(scan_prefix(after(pay, column)))
-    column = after(column, pay)
-    stats = far_stats(codes, me, near, column, qos)
+    pay = exchange(after(pay, shifted[0], shifted[1], near, listed))
+    carried = scan_prefix(pay)
+    column = after(column, qos)
+    carried = exchange(after(carried, column))
+    stats = far_stats(listed, near, column, qos)
     stats = jnp.stack([stats] + [along_x(stats, d) for d in range(1, NX)])
-    stats = after(stats, carried)
-    kv_far, dq_far = far_grads(codes, me, stats, column, qos)
+    kv_far, ds_far = far_grads(listed, me, stats, column, qos)
     kv_far = lax.psum_scatter(
-        kv_far, "seq", scatter_dimension=0, axis_index_groups=Z_GROUPS
-    )
-    carried = after(carried, dq_far)
-    dq_far = exchange(dq_far, X_GROUPS)
+        after(kv_far, carried), "seq", scatter_dimension=0, axis_index_groups=Z_GROUPS
+    )
+    dq_far = far_queries(listed, me, ds_far, column)
     dx, dl, bc = scan_grads(x, g, ld, b, c, ends, starts, carried)
     shares = lax.all_to_all(bc.reshape(8, 128, NST), "head", 0, 0, tiled=True)
+    dq_far = exchange(after(dq_far, bc), X_GROUPS)
     part = jnp.sum(shares.astype(F32), axis=0).astype(BF16)
     whole = lax.all_gather(part, "head", tiled=True).astype(F32)
-    dq_near, kv_near = near_grads(me, after(stats, dq_far), qo, kv)
-    dq = (dq_near + jnp.sum(dq_far.astype(F32), axis=0)).astype(BF16)
-    kv_grad = (kv_near + kv_far.astype(F32).reshape(kv_near.shape)).astype(BF16)
+    dq, kv_near = near_grads(me, stats, qo, kv, dq_far)
+    dk, dv = finish(kv_near, kv_far)
     return (
-        jnp.swapaxes(dq, 0, 1),
-        jnp.swapaxes(kv_grad[:, 0], 0, 1),
-        jnp.swapaxes(kv_grad[:, 1], 0, 1),
+        dq.reshape(q.shape),
+        dk.reshape(k.shape),
+        dv.reshape(v.shape),
         dx,
         dl,
         whole[:TOK],

time: 192 us -> 181 us (0.943)
  blocking collectives: 59.3 us -> 13.6 us
  waiting for transfers between devices: 36.3 us -> 50.8 us
  starting transfers between devices: 21.5 us -> 33.2 us
  Pallas kernels: 39.4 us -> 47.3 us
  local copies, waits for them, and re-layouts: 14.7 us -> 17.8 us
  other arithmetic: 6.18 us -> 3.27 us
    all_to_all x2 -> x0, blocking collectives: 45.3 us -> none  [the longest x1 33.5 us: exchange(): lax.all_to_all(value, 'seq', 0, 0, tiled=True, axis_index_groups=groups)]
    all_gather x1, waiting for transfers between devices: 5.67 us -> 19.9 us  [per_device(): column = lax.all_gather(kv, 'seq', axis_index_groups=Z_GROUPS)]
    all_to_all x2 -> x3, waiting for transfers between devices: 0.01 us -> 8.82 us  [exchange(): lax.all_to_all(value, 'seq', 0, 0, tiled=True, axis_index_groups=groups)]
    pallas_call x4 -> x8, Pallas kernels: 21.5 us -> 29 us  [the longest x1 10.5 us: far_grads(): call(far_grads_body, 'far_grads', [((NZ, 2 * TOK, PAIR), BF16, pltpu.HBM)...]
    ppermute x6 -> x7, waiting for transfers between devices: 27.1 us -> 20 us  [along_x(): return lax.ppermute(value, 'seq', pairs)]
    all_to_all x2 -> x3, starting transfers between devices: 12.3 us -> 18.9 us  [exchange(): lax.all_to_all(value, 'seq', 0, 0, tiled=True, axis_index_groups=groups)]
    all_to_all x0 -> x1, starting transfers between devices: none -> 4.92 us  [per_device(): shares = lax.all_to_all(bc.reshape(8, 128, NST), 'head', 0, 0, tiled=True)]
    unnamed x53 -> x48, local copies, waits for them, and re-layouts: 9.79 us -> 14.1 us
  transfers between devices with their start and end apart: 10 -> 13, of which waited for: 8 -> 9; matrix products, arithmetic and copies ran while one was open for 4% -> 4% of each run, Pallas kernels for 13% -> 25%
where the time goes in v1:
time: 181 us; the launch traced here: 180 us
  waiting for transfers between devices  50.8 us (28%)
  Pallas kernels  47.3 us (26%)
  starting transfers between devices  33.2 us (18%)
  local copies, waits for them, and re-layouts  17.8 us (10%)
  between operations  14.4 us (8%)
  blocking collectives  13.6 us (8%)
  other arithmetic  3.27 us (2%)
    ppermute x7, waiting for transfers between devices, along_x(): return lax.ppermute(value, 'seq', pairs)  20 us
    all_gather x1, waiting for transfers between devices, per_device(): column = lax.all_gather(kv, 'seq', axis_index_groups=Z_GROUPS)  19.9 us
    all_to_all x3, starting transfers between devices, exchange(): lax.all_to_all(value, 'seq', 0, 0, tiled=True, axis_index_groups=groups)  18.9 us
    unnamed x48, local copies, waits for them, and re-layouts  14.1 us
    all_gather x1, blocking collectives, per_device(): whole = lax.all_gather(part, 'head', tiled=True).astype(F32)  13.6 us
    pallas_call x1, Pallas kernels, scan_grads(): call(grads_body, 'scan_grads', [((TOK, WIDTH), BF16, vm), ((TOK, SH), F32...  12.7 us
    pallas_call x1, Pallas kernels, far_grads(): call(far_grads_body, 'far_grads', [((NZ, 2 * TOK, PAIR), BF16, pltpu.HBM)...  10.5 us
    ppermute x7, starting transfers between devices, along_x(): return lax.ppermute(value, 'seq', pairs)  9.26 us
  transfers between devices with their start and end apart: 13, of which 9 were waited for; matrix products, arithmetic and copies ran while one was open for 4% of the time, Pallas kernels for 25%

profile of v1, /device:TPU:1, one launch (start us, length us, event | category | flops | bytes accessed | tf_op | source)
XLA Modules:
  0.0 180.3 jit_solution(13391963125922523774)
XLA Ops:
  12.2 3.4 %collective-permute-start.2 = (bf16[2,512,256]{2,1,0:T(8,128)(2,1)S(1)}, bf16[2,512,256]{2,1,0:T(8,128)(2,1)}, u32[]{:S(2)}, u32[]{:S(2)}) collective-permute-start(bf16[2,512,256]{2,1,0:T(8,128)(2,1)S(1)} %by_head.2.qo), channel_id=1, source_target_pairs={{0,192},{8,200},{16,208},{24,216},{32,224},{40,232},{48,240},{56,2... | collective-permute-start | bytes 1572872 | tf_op jit(solution)/shard_map/ppermute | solution.py:708
  17.4 2.1 %near_stats.1.near = f32[8,512]{1,0:T(8,128)S(1)} custom-call(bf16[2,512,256]{2,1,0:T(8,128)(2,1)S(1)} %by_head.2.qo, bf16[2,512,256]{2,1,0:T(8,128)(2,1)} %by_head.3.kv), custom_call_target="tpu_custom_call" | custom-call | flops 268435456 | bytes 1048576 | tf_op jit(solution)/shard_map/near_stats/pallas_call | solution.py:154
  19.7 4.6 %scan_ends.1 = (f32[4,1024,128]{2,1,0:T(8,128)S(1)}, f32[4,1024,128]{2,1,0:T(8,128)}, bf16[32,80,128]{2,1,0:T(8,128)(2,1)}) custom-call(bf16[512,1024]{1,0:T(8,128)(2,1)S(1)} %copy-done.9, bf16[512,1024]{1,0:T(8,128)(2,1)S(1)} %copy-done.11, f32[512,16]{1,0:T(8,128)S(1)} %copy.33.ld_ref, bf16[512,128]{1,0:T(8,128)(2,1)S(1)} %copy-done.13, ...), custom_call_target="tpu_custom_call" | custom-call | flops 1073741824 | bytes 8388608 | tf_op jit(solution)/shard_map/scan_ends/pallas_call | solution.py:563
  24.3 1.3 copy-done.17
  26.4 2.9 %collective-permute-done = bf16[2,512,256]{2,1,0:T(8,128)(2,1)} collective-permute-done((bf16[2,512,256]{2,1,0:T(8,128)(2,1)S(1)}, bf16[2,512,256]{2,1,0:T(8,128)(2,1)}, u32[]{:S(2)}, u32[]{:S(2)}) %collective-permute-start) | collective-permute-done | bytes 524320 | tf_op jit(solution)/shard_map/ppermute | solution.py:708
  29.4 8.6 %all-to-all-start = ((bf16[32,80,128]{2,1,0:T(8,128)(2,1)}), bf16[32,80,128]{2,1,0:T(8,128)(2,1)S(1)}, u32[]{:S(2)}, u32[]{:S(2)}) async-start(bf16[32,80,128]{2,1,0:T(8,128)(2,1)} %get-tuple-element.29), calls=%async_computation | async-start | bytes 1310720 | tf_op jit(solution)/shard_map/all_to_all | solution.py:701
  38.0 1.0 slice.19
  39.0 2.6 %collective-permute-start.3 = (bf16[1,512,256]{2,1,0:T(8,128)(2,1)S(1)}, bf16[1,512,256]{2,1,0:T(8,128)(2,1)S(1)}, u32[]{:S(2)}, u32[]{:S(2)}) collective-permute-start(bf16[1,512,256]{2,1,0:T(8,128)(2,1)S(1)} %slice.19), channel_id=1, source_target_pairs={{0,192},{8,200},{16,208},{24,216},{32,224},{40,232},{48,240},{56,2... | collective-permute-start | bytes 786440 | tf_op jit(solution)/shard_map/ppermute | solution.py:708
  41.5 1.0 slice.18
  42.6 5.1 %collective-permute-done.3 = bf16[1,512,256]{2,1,0:T(8,128)(2,1)S(1)} collective-permute-done((bf16[1,512,256]{2,1,0:T(8,128)(2,1)S(1)}, bf16[1,512,256]{2,1,0:T(8,128)(2,1)S(1)}, u32[]{:S(2)}, u32[]{:S(2)}) %collective-permute-start.3) | collective-permute-done | bytes 262176 | tf_op jit(solution)/shard_map/ppermute | solution.py:708
  47.7 3.3 %collective-permute-done.1 = bf16[1,512,256]{2,1,0:T(8,128)(2,1)S(1)} collective-permute-done((bf16[1,512,256]{2,1,0:T(8,128)(2,1)S(1)}, bf16[1,512,256]{2,1,0:T(8,128)(2,1)S(1)}, u32[]{:S(2)}, u32[]{:S(2)}) %collective-permute-start.1) | collective-permute-done | bytes 262176 | tf_op jit(solution)/shard_map/ppermute | solution.py:708
  51.1 1.5 pad_maximum_fusion.qos_in
  52.5 8.8 %all-to-all-done.inp = bf16[32,80,128]{2,1,0:T(8,128)(2,1)S(1)} async-done(((bf16[32,80,128]{2,1,0:T(8,128)(2,1)}), bf16[32,80,128]{2,1,0:T(8,128)(2,1)S(1)}, u32[]{:S(2)}, u32[]{:S(2)}) %all-to-all-start) | async-done | bytes 655392 | tf_op jit(solution)/shard_map/all_to_all | solution.py:701
  63.1 19.9 %all-gather.3.cloned.1.call-done = bf16[16,512,256]{2,1,0:T(8,128)(2,1)} async-done(((bf16[2,512,256]{2,1,0:T(8,128)(2,1)}), bf16[16,512,256]{2,1,0:T(8,128)(2,1)}) %all-gather.3.cloned.1.call-update) | async-done | bytes 4194320 | tf_op jit(solution)/shard_map/all_gather | solution.py:718
  83.0 6.8 %all-to-all-start.1 = ((bf16[32,64,128]{2,1,0:T(8,128)(2,1)}), bf16[32,64,128]{2,1,0:T(8,128)(2,1)S(1)}, u32[]{:S(2)}, u32[]{:S(2)}) async-start(bf16[32,64,128]{2,1,0:T(8,128)(2,1)} %copy-done.1), calls=%async_computation.1 | async-start | bytes 1048576 | tf_op jit(solution)/shard_map/all_to_all | solution.py:701
  89.9 5.6 %far_stats.1 = f32[5,8,512]{2,1,0:T(8,128)S(1)} custom-call(s32[137]{0:T(256)S(1)} %pad_add_fusion.listed, f32[8,512]{1,0:T(8,128)S(1)} %near_stats.1.near, bf16[8,2,512,256]{3,2,1,0:T(8,128)(2,1)} %bitcast.23, bf16[4,2,512,256]{3,2,1,0:T(8,128)(2,1)S(1)} %pad_maximum_fusion.qos_in), custom_call_target="tpu_custom_call" | custom-call | flops 268435456 | bytes 6291456 | tf_op jit(solution)/shard_map/far_stats/pallas_call | solution.py:241
  95.5 2.5 %collective-permute-start.6 = (f32[5,8,512]{2,1,0:T(8,128)S(1)}, f32[5,8,512]{2,1,0:T(8,128)S(1)}, u32[]{:S(2)}, u32[]{:S(2)}) collective-permute-start(f32[5,8,512]{2,1,0:T(8,128)S(1)} %far_stats.1), channel_id=1, source_target_pairs={{0,192},{8,200},{16,208},{24,216},{32,224},{40,232},{48,240},{56,2... | collective-permute-start | bytes 245768 | tf_op jit(solution)/shard_map/ppermute | solution.py:708
  98.7 2.1 %collective-permute-done.6 = f32[5,8,512]{2,1,0:T(8,128)S(1)} collective-permute-done((f32[5,8,512]{2,1,0:T(8,128)S(1)}, f32[5,8,512]{2,1,0:T(8,128)S(1)}, u32[]{:S(2)}, u32[]{:S(2)}) %collective-permute-start.6) | collective-permute-done | bytes 81952 | tf_op jit(solution)/shard_map/ppermute | solution.py:708
  100.8 2.6 %collective-permute-done.5 = f32[5,8,512]{2,1,0:T(8,128)S(1)} collective-permute-done((f32[5,8,512]{2,1,0:T(8,128)S(1)}, f32[5,8,512]{2,1,0:T(8,128)S(1)}, u32[]{:S(2)}, u32[]{:S(2)}) %collective-permute-start.5) | collective-permute-done | bytes 81952 | tf_op jit(solution)/shard_map/ppermute | solution.py:708
  103.4 3.9 %collective-permute-done.4 = f32[5,8,512]{2,1,0:T(8,128)S(1)} collective-permute-done((f32[5,8,512]{2,1,0:T(8,128)S(1)}, f32[5,8,512]{2,1,0:T(8,128)S(1)}, u32[]{:S(2)}, u32[]{:S(2)}) %collective-permute-start.4) | collective-permute-done | bytes 81952 | tf_op jit(solution)/shard_map/ppermute | solution.py:708
  107.3 10.5 %far_grads.1 = (bf16[8,1024,256]{2,1,0:T(8,128)(2,1)}, bf16[68,128,256]{2,1,0:T(8,128)(2,1)}) custom-call(s32[137]{0:T(256)S(1)} %pad_add_fusion.listed, s32[1]{0:T(128)} %bitcast.me, f32[4,5,8,512]{3,2,1,0:T(8,128)S(1)} %pad_maximum_fusion.1.stats, bf16[8,2,512,256]{3,2,1,0:T(8,128)(2,1)} %bitcast.24, bf16[4,2,512,256]{3,2,1,0:T(8,128)(2,1)S(1)} %pad_maximum_fusion.qos_in), custom_call_target="tpu_custom_call" | custom-call | flops 536870912 | bytes 12582912 | tf_op jit(solution)/shard_map/far_grads/pallas_call | solution.py:337
  119.2 1.2 copy-done.12
  120.5 1.6 copy-done.18
  122.1 12.7 %scan_grads.1 = (bf16[512,1024]{1,0:T(8,128)(2,1)}, f32[512,16]{1,0:T(8,128)S(1)}, bf16[1024,128]{1,0:T(8,128)(2,1)}) custom-call(bf16[512,1024]{1,0:T(8,128)(2,1)S(1)} %copy-done.10, bf16[512,1024]{1,0:T(8,128)(2,1)S(1)} %copy-done.12, f32[512,16]{1,0:T(8,128)S(1)} %copy-done.4, bf16[512,128]{1,0:T(8,128)(2,1)S(1)} %copy-done.14, ...), custom_call_target="tpu_custom_call" | custom-call | flops 4294967296 | bytes 12582912 | tf_op jit(solution)/shard_map/scan_grads/pallas_call | solution.py:680
  134.8 4.9 %all-to-all-start.3 = ((bf16[8,128,128]{2,1,0:T(8,128)(2,1)}), bf16[8,128,128]{2,1,0:T(8,128)(2,1)S(1)}, u32[]{:S(2)}, u32[]{:S(2)}) async-start(bf16[8,128,128]{2,1,0:T(8,128)(2,1)} %bitcast.20), calls=%async_computation.4 | async-start | bytes 524288 | tf_op jit(solution)/shard_map/all_to_all | solution.py:740
  139.7 2.2 %copy-done = bf16[16,512,256]{2,1,0:T(8,128)(2,1)S(1)} copy-done((bf16[16,512,256]{2,1,0:T(8,128)(2,1)S(1)}, bf16[16,512,256]{2,1,0:T(8,128)(2,1)}, u32[]{:S(2)}) %copy-start) | copy-done | bytes 4194328
  141.9 4.3 %far_queries.1 = bf16[4,512,256]{2,1,0:T(8,128)(2,1)} custom-call(s32[137]{0:T(256)S(1)} %pad_add_fusion.listed, s32[1]{0:T(128)} %bitcast.me, bf16[68,128,256]{2,1,0:T(8,128)(2,1)} %get-tuple-element.25.ds_in, bf16[8,2,512,256]{3,2,1,0:T(8,128)(2,1)S(1)} %bitcast.25), custom_call_target="tpu_custom_call" | custom-call | flops 134217728 | bytes 6291456 | tf_op jit(solution)/shard_map/far_queries/pallas_call | solution.py:398
  146.3 3.5 %all-to-all-start.2 = ((bf16[4,512,256]{2,1,0:T(8,128)(2,1)}), bf16[4,512,256]{2,1,0:T(8,128)(2,1)S(1)}, u32[]{:S(2)}, u32[]{:S(2)}) async-start(bf16[4,512,256]{2,1,0:T(8,128)(2,1)} %far_queries.1), calls=%async_computation.2 | async-start | bytes 2097152 | tf_op jit(solution)/shard_map/all_to_all | solution.py:701
  150.6 13.6 %all_gather.11 = bf16[1024,128]{1,0:T(8,128)(2,1)S(1)} all-gather(bf16[128,128]{1,0:T(8,128)(2,1)S(1)} %reduce_sum.52), channel_id=1, replica_groups=mesh['seq'=32,'head'=8] {'head'}, dimensions={0}, use_global_device_ids=true | all-gather | bytes 294912 | tf_op jit(solution)/shard_map/all_gather | solution.py:743
  165.0 4.5 %near_grads.1 = (bf16[1024,128]{1,0:T(8,128)(2,1)}, f32[2,512,256]{2,1,0:T(8,128)S(1)}) custom-call(s32[1]{0:T(128)} %bitcast.me, f32[4,5,8,512]{3,2,1,0:T(8,128)S(1)} %pad_maximum_fusion.1.stats, bf16[2,512,256]{2,1,0:T(8,128)(2,1)S(1)} %by_head.2.qo, bf16[2,512,256]{2,1,0:T(8,128)(2,1)} %by_head.3.kv, bf16[4,512,256]{2,1,0:T(8,128)(2,1)S(1)} %all-to-all-done.2.dq_far), custom_call_target="tpu_custom_call" | custom-call | flops 671088640 | bytes 4194304 | tf_op jit(solution)/shard_map/near_grads/pallas_call | solution.py:445
  169.5 2.1 %reduce-scatter.2.cloned.1.call-done = bf16[1,1024,256]{2,1,0:T(8,128)(2,1)} async-done(((bf16[8,1024,256]{2,1,0:T(8,128)(2,1)}), bf16[1,1024,256]{2,1,0:T(8,128)(2,1)}) %reduce-scatter.2.cloned.1.call-update) | async-done | bytes 524304 | tf_op jit(solution)/shard_map/reduce_scatter | solution.py:735
  171.6 1.0 copy-done.2
  (78 shorter events, 14.1 us)
Async XLA Ops:
  7.2 8.4 %copy-start.20 = (s32[128,4]{0,1:T(4,128)S(1)}, s32[128,4]{0,1:T(4,128)}, u32[]{:S(2)}) copy-start(s32[128,4]{0,1:T(4,128)} %param.22) | copy-start | bytes 6148
  7.2 8.4 %copy-start.22 = (s32[128]{0:T(128)S(1)}, s32[128]{0:T(128)}, u32[]{:S(2)}) copy-start(s32[128]{0:T(128)} %param.23) | copy-start | bytes 1540
  7.2 75.8 %all-gather.3.cloned.1.call-start = ((), (), s32[]{:S(2)}) async-start(), calls=%async_computation.6 | async-start | bytes 4718592 | tf_op jit(solution)/shard_map/all_gather | solution.py:718
  9.1 6.5 %copy-start.21 = (s32[128,4]{0,1:T(4,128)S(1)}, s32[128,4]{0,1:T(4,128)}, u32[]{:S(2)}) copy-start(s32[128,4]{0,1:T(4,128)} %param.21) | copy-start | bytes 6148
  9.1 8.1 %copy-start.19 = (f32[512,16]{0,1:T(8,128)S(1)}, f32[512,16]{0,1:T(8,128)}, u32[]{:S(2)}) copy-start(f32[512,16]{0,1:T(8,128)} %param.17) | copy-start | bytes 98308
  9.1 10.5 %copy-start.9 = (bf16[512,1024]{1,0:T(8,128)(2,1)S(1)}, bf16[512,1024]{1,0:T(8,128)(2,1)}, u32[]{:S(2)}) copy-start(bf16[512,1024]{1,0:T(8,128)(2,1)} %x_ref.3) | copy-start | bytes 3145732
  9.1 10.5 %copy-start.13 = (bf16[512,128]{1,0:T(8,128)(2,1)S(1)}, bf16[512,128]{1,0:T(8,128)(2,1)}, u32[]{:S(2)}) copy-start(bf16[512,128]{1,0:T(8,128)(2,1)} %b_ref.3) | copy-start | bytes 393220
  9.1 10.5 %copy-start.15 = (bf16[512,128]{1,0:T(8,128)(2,1)S(1)}, bf16[512,128]{1,0:T(8,128)(2,1)}, u32[]{:S(2)}) copy-start(bf16[512,128]{1,0:T(8,128)(2,1)} %c_ref.3) | copy-start | bytes 393220
  10.1 1.0 copy-start.7
  12.0 7.6 %copy-start.11 = (bf16[512,1024]{1,0:T(8,128)(2,1)S(1)}, bf16[512,1024]{1,0:T(8,128)(2,1)}, u32[]{:S(2)}) copy-start(bf16[512,1024]{1,0:T(8,128)(2,1)} %g_ref.3) | copy-start | bytes 3145732
  12.2 14.2 %collective-permute-start.2 = (bf16[2,512,256]{2,1,0:T(8,128)(2,1)S(1)}, bf16[2,512,256]{2,1,0:T(8,128)(2,1)}, u32[]{:S(2)}, u32[]{:S(2)}) collective-permute-start(bf16[2,512,256]{2,1,0:T(8,128)(2,1)S(1)} %by_head.2.qo), channel_id=1, source_target_pairs={{0,192},{8,200},{16,208},{24,216},{32,224},{40,232},{48,240},{56,2... | collective-permute-start | bytes 1572872 | tf_op jit(solution)/shard_map/ppermute | solution.py:708
  15.6 13.8 %collective-permute-start = (bf16[2,512,256]{2,1,0:T(8,128)(2,1)S(1)}, bf16[2,512,256]{2,1,0:T(8,128)(2,1)}, u32[]{:S(2)}, u32[]{:S(2)}) collective-permute-start(bf16[2,512,256]{2,1,0:T(8,128)(2,1)S(1)} %by_head.2.qo), channel_id=1, source_target_pairs={{0,64},{8,72},{16,80},{24,88},{32,96},{40,104},{48,112},{56,120},{... | collective-permute-start | bytes 1572872 | tf_op jit(solution)/shard_map/ppermute | solution.py:708
  17.4 6.9 %copy-start.3 = (f32[512,16]{1,0:T(8,128)}, f32[512,16]{1,0:T(8,128)S(1)}, u32[]{:S(2)}) copy-start(f32[512,16]{1,0:T(8,128)S(1)} %copy.33.ld_ref) | copy-start | bytes 98308
  24.3 1.3 copy-start.17
  29.4 32.0 %all-to-all-start = ((bf16[32,80,128]{2,1,0:T(8,128)(2,1)}), bf16[32,80,128]{2,1,0:T(8,128)(2,1)S(1)}, u32[]{:S(2)}, u32[]{:S(2)}) async-start(bf16[32,80,128]{2,1,0:T(8,128)(2,1)} %get-tuple-element.29), calls=%async_computation | async-start | bytes 1310720 | tf_op jit(solution)/shard_map/all_to_all | solution.py:701
  39.0 8.7 %collective-permute-start.3 = (bf16[1,512,256]{2,1,0:T(8,128)(2,1)S(1)}, bf16[1,512,256]{2,1,0:T(8,128)(2,1)S(1)}, u32[]{:S(2)}, u32[]{:S(2)}) collective-permute-start(bf16[1,512,256]{2,1,0:T(8,128)(2,1)S(1)} %slice.19), channel_id=1, source_target_pairs={{0,192},{8,200},{16,208},{24,216},{32,224},{40,232},{48,240},{56,2... | collective-permute-start | bytes 786440 | tf_op jit(solution)/shard_map/ppermute | solution.py:708
  42.5 8.5 %collective-permute-start.1 = (bf16[1,512,256]{2,1,0:T(8,128)(2,1)S(1)}, bf16[1,512,256]{2,1,0:T(8,128)(2,1)S(1)}, u32[]{:S(2)}, u32[]{:S(2)}) collective-permute-start(bf16[1,512,256]{2,1,0:T(8,128)(2,1)S(1)} %slice.18), channel_id=1, source_target_pairs={{0,64},{8,72},{16,80},{24,88},{32,96},{40,104},{48,112},{56,120},{... | collective-permute-start | bytes 786440 | tf_op jit(solution)/shard_map/ppermute | solution.py:708
  83.0 34.9 %all-to-all-start.1 = ((bf16[32,64,128]{2,1,0:T(8,128)(2,1)}), bf16[32,64,128]{2,1,0:T(8,128)(2,1)S(1)}, u32[]{:S(2)}, u32[]{:S(2)}) async-start(bf16[32,64,128]{2,1,0:T(8,128)(2,1)} %copy-done.1), calls=%async_computation.1 | async-start | bytes 1048576 | tf_op jit(solution)/shard_map/all_to_all | solution.py:701
  89.8 81.8 %reduce-scatter.2.cloned.1.call-start = ((), (), s32[]{:S(2)}) async-start(), calls=%async_computation.5 | async-start | bytes 4718592 | tf_op jit(solution)/shard_map/reduce_scatter | solution.py:735
  95.5 5.3 %collective-permute-start.6 = (f32[5,8,512]{2,1,0:T(8,128)S(1)}, f32[5,8,512]{2,1,0:T(8,128)S(1)}, u32[]{:S(2)}, u32[]{:S(2)}) collective-permute-start(f32[5,8,512]{2,1,0:T(8,128)S(1)} %far_stats.1), channel_id=1, source_target_pairs={{0,192},{8,200},{16,208},{24,216},{32,224},{40,232},{48,240},{56,2... | collective-permute-start | bytes 245768 | tf_op jit(solution)/shard_map/ppermute | solution.py:708
  98.0 5.4 %collective-permute-start.5 = (f32[5,8,512]{2,1,0:T(8,128)S(1)}, f32[5,8,512]{2,1,0:T(8,128)S(1)}, u32[]{:S(2)}, u32[]{:S(2)}) collective-permute-start(f32[5,8,512]{2,1,0:T(8,128)S(1)} %far_stats.1), channel_id=1, source_target_pairs={{0,128},{8,136},{16,144},{24,152},{32,160},{40,168},{48,176},{56,1... | collective-permute-start | bytes 245768 | tf_op jit(solution)/shard_map/ppermute | solution.py:708
  98.0 9.3 %collective-permute-start.4 = (f32[5,8,512]{2,1,0:T(8,128)S(1)}, f32[5,8,512]{2,1,0:T(8,128)S(1)}, u32[]{:S(2)}, u32[]{:S(2)}) collective-permute-start(f32[5,8,512]{2,1,0:T(8,128)S(1)} %far_stats.1), channel_id=1, source_target_pairs={{0,64},{8,72},{16,80},{24,88},{32,96},{40,104},{48,112},{56,120},{... | collective-permute-start | bytes 245768 | tf_op jit(solution)/shard_map/ppermute | solution.py:708
  117.9 1.0 copy-start.4
  117.9 1.3 copy-start.10
  117.9 1.3 copy-start.14
  117.9 1.3 copy-start.16
  119.2 1.2 copy-start.12
  120.5 1.6 copy-start.18
  134.8 11.5 %all-to-all-start.3 = ((bf16[8,128,128]{2,1,0:T(8,128)(2,1)}), bf16[8,128,128]{2,1,0:T(8,128)(2,1)S(1)}, u32[]{:S(2)}, u32[]{:S(2)}) async-start(bf16[8,128,128]{2,1,0:T(8,128)(2,1)} %bitcast.20), calls=%async_computation.4 | async-start | bytes 524288 | tf_op jit(solution)/shard_map/all_to_all | solution.py:740
  139.7 2.2 %copy-start = (bf16[16,512,256]{2,1,0:T(8,128)(2,1)S(1)}, bf16[16,512,256]{2,1,0:T(8,128)(2,1)}, u32[]{:S(2)}) copy-start(bf16[16,512,256]{2,1,0:T(8,128)(2,1)} %all-gather.3.cloned.1.call-done) | copy-start | bytes 12582916
  146.3 18.7 %all-to-all-start.2 = ((bf16[4,512,256]{2,1,0:T(8,128)(2,1)}), bf16[4,512,256]{2,1,0:T(8,128)(2,1)S(1)}, u32[]{:S(2)}, u32[]{:S(2)}) async-start(bf16[4,512,256]{2,1,0:T(8,128)(2,1)} %far_queries.1), calls=%async_computation.2 | async-start | bytes 2097152 | tf_op jit(solution)/shard_map/all_to_all | solution.py:701
  171.6 1.0 copy-start.2
  (4 other events, 3.7 us)
Sparse Core Ops, SparseCore 0:
  10.3 72.7 all-gather.2
  118.1 53.4 reduce-scatter.1

commit v2 on v1

--- a/solution.py
+++ b/solution.py
@@ -719,16 +719,15 @@
     qo = by_head(q, o)
     live = jnp.arange(GLOB)[None, :] < count[:, None]
     codes = jnp.where(live, owner * SEG + offset, -1).reshape(NS * ITEMS)
-    listed = far_items(codes, me)
     shifted = [along_x(qo, 1), along_x(qo, 3)]
-    opposite = jnp.concatenate([along_x(shifted[0][:1], 1), along_x(shifted[1][1:], 3)])
+    opposite = [along_x(shifted[0][:1], 1), along_x(shifted[1][1:], 3)]
+    ends, starts, pay = scan_ends(x, g, ld, b, c)
+    pay = exchange(after(pay, shifted[0], shifted[1]))
+    listed = far_items(after(codes, pay), me)
+    opposite = jnp.concatenate(after(opposite, pay))
     qos = jnp.stack([qo, shifted[0], opposite, shifted[1]])
-    near = near_stats(qo, kv)
-    ends, starts, pay = scan_ends(x, g, ld, b, c)
-    pay = exchange(after(pay, shifted[0], shifted[1], near, listed))
-    carried = scan_prefix(pay)
-    column = after(column, qos)
-    carried = exchange(after(carried, column))
+    near = near_stats(after(qo, pay), kv)
+    carried = exchange(scan_prefix(after(pay, near, listed, qos)))
     stats = far_stats(listed, near, column, qos)
     stats = jnp.stack([stats] + [along_x(stats, d) for d in range(1, NX)])
     kv_far, ds_far = far_grads(listed, me, stats, column, qos)

time: 181 us -> 173 us (0.956)
  waiting for transfers between devices: 50.8 us -> 37.1 us
  starting transfers between devices: 33.2 us -> 36.3 us
  local copies, waits for them, and re-layouts: 17.8 us -> 20.6 us
  Pallas kernels: 47.3 us -> 45.4 us
    all_gather x1, waiting for transfers between devices: 19.9 us -> 5.34 us  [per_device(): column = lax.all_gather(kv, 'seq', axis_index_groups=Z_GROUPS)]
    unnamed x48, local copies, waits for them, and re-layouts: 14.1 us -> 16.8 us
  transfers between devices with their start and end apart: 13 -> 13, of which waited for: 9 -> 11; matrix products, arithmetic and copies ran while one was open for 4% -> 5% of each run, Pallas kernels for 25% -> 25%
where the time goes in v2:
time: 173 us; the launch traced here: 171 us
  Pallas kernels  45.4 us (26%)
  waiting for transfers between devices  37.1 us (21%)
  starting transfers between devices  36.3 us (21%)
  local copies, waits for them, and re-layouts  20.6 us (12%)
  between operations  14.3 us (8%)
  blocking collectives  13.7 us (8%)
  other arithmetic  3.85 us (2%)
    all_to_all x3, starting transfers between devices, exchange(): lax.all_to_all(value, 'seq', 0, 0, tiled=True, axis_index_groups=groups)  20.4 us
    ppermute x7, waiting for transfers between devices, along_x(): return lax.ppermute(value, 'seq', pairs)  19.6 us
    unnamed x48, local copies, waits for them, and re-layouts  16.8 us
    all_gather x1, blocking collectives, per_device(): whole = lax.all_gather(part, 'head', tiled=True).astype(F32)  13.7 us
    pallas_call x1, Pallas kernels, scan_grads(): call(grads_body, 'scan_grads', [((TOK, WIDTH), BF16, vm), ((TOK, SH), F32...  12.8 us
    all_to_all x3, waiting for transfers between devices, exchange(): lax.all_to_all(value, 'seq', 0, 0, tiled=True, axis_index_groups=groups)  10.3 us
    ppermute x7, starting transfers between devices, along_x(): return lax.ppermute(value, 'seq', pairs)  9.64 us
    pallas_call x1, Pallas kernels, far_grads(): call(far_grads_body, 'far_grads', [((NZ, 2 * TOK, PAIR), BF16, pltpu.HBM)...  9.45 us
  transfers between devices with their start and end apart: 13, of which 11 were waited for; matrix products, arithmetic and copies ran while one was open for 5% of the time, Pallas kernels for 25%

profile of v2, /device:TPU:1, one launch (start us, length us, event | category | flops | bytes accessed | tf_op | source)
XLA Modules:
  0.0 171.2 jit_solution(5083188907528630191)
XLA Ops:
  12.2 3.4 %collective-permute-start.1 = (bf16[2,512,256]{2,1,0:T(8,128)(2,1)S(1)}, bf16[2,512,256]{2,1,0:T(8,128)(2,1)}, u32[]{:S(2)}, u32[]{:S(2)}) collective-permute-start(bf16[2,512,256]{2,1,0:T(8,128)(2,1)S(1)} %by_head.2.qo), channel_id=1, source_target_pairs={{0,192},{8,200},{16,208},{24,216},{32,224},{40,232},{48,240},{56,2... | collective-permute-start | bytes 1572872 | tf_op jit(solution)/shard_map/ppermute | solution.py:708
  15.7 1.2 copy-done.11
  16.9 4.6 %scan_ends.1 = (f32[4,1024,128]{2,1,0:T(8,128)S(1)}, f32[4,1024,128]{2,1,0:T(8,128)}, bf16[32,80,128]{2,1,0:T(8,128)(2,1)}) custom-call(bf16[512,1024]{1,0:T(8,128)(2,1)S(1)} %copy-done.9, bf16[512,1024]{1,0:T(8,128)(2,1)S(1)} %copy-done.11, f32[512,16]{1,0:T(8,128)S(1)} %copy.31.ld_ref, bf16[512,128]{1,0:T(8,128)(2,1)S(1)} %copy-done.13, ...), custom_call_target="tpu_custom_call" | custom-call | flops 1073741824 | bytes 8388608 | tf_op jit(solution)/shard_map/scan_ends/pallas_call | solution.py:563
  21.5 1.3 copy-done.17
  22.8 3.3 %collective-permute-done.1 = bf16[2,512,256]{2,1,0:T(8,128)(2,1)} collective-permute-done((bf16[2,512,256]{2,1,0:T(8,128)(2,1)S(1)}, bf16[2,512,256]{2,1,0:T(8,128)(2,1)}, u32[]{:S(2)}, u32[]{:S(2)}) %collective-permute-start.1) | collective-permute-done | bytes 524320 | tf_op jit(solution)/shard_map/ppermute | solution.py:708
  26.1 3.2 %collective-permute-done = bf16[2,512,256]{2,1,0:T(8,128)(2,1)} collective-permute-done((bf16[2,512,256]{2,1,0:T(8,128)(2,1)S(1)}, bf16[2,512,256]{2,1,0:T(8,128)(2,1)}, u32[]{:S(2)}, u32[]{:S(2)}) %collective-permute-start) | collective-permute-done | bytes 524320 | tf_op jit(solution)/shard_map/ppermute | solution.py:708
  29.3 8.6 %all-to-all-start = ((bf16[32,80,128]{2,1,0:T(8,128)(2,1)}), bf16[32,80,128]{2,1,0:T(8,128)(2,1)S(1)}, u32[]{:S(2)}, u32[]{:S(2)}) async-start(bf16[32,80,128]{2,1,0:T(8,128)(2,1)} %get-tuple-element.28), calls=%async_computation | async-start | bytes 1310720 | tf_op jit(solution)/shard_map/all_to_all | solution.py:701
  39.0 2.6 %collective-permute-start.3 = (bf16[1,512,256]{2,1,0:T(8,128)(2,1)S(1)}, bf16[1,512,256]{2,1,0:T(8,128)(2,1)S(1)}, u32[]{:S(2)}, u32[]{:S(2)}) collective-permute-start(bf16[1,512,256]{2,1,0:T(8,128)(2,1)S(1)} %slice.19), channel_id=1, source_target_pairs={{0,192},{8,200},{16,208},{24,216},{32,224},{40,232},{48,240},{56,2... | collective-permute-start | bytes 786440 | tf_op jit(solution)/shard_map/ppermute | solution.py:708
  42.9 4.9 %collective-permute-done.3 = bf16[1,512,256]{2,1,0:T(8,128)(2,1)S(1)} collective-permute-done((bf16[1,512,256]{2,1,0:T(8,128)(2,1)S(1)}, bf16[1,512,256]{2,1,0:T(8,128)(2,1)S(1)}, u32[]{:S(2)}, u32[]{:S(2)}) %collective-permute-start.3) | collective-permute-done | bytes 262176 | tf_op jit(solution)/shard_map/ppermute | solution.py:708
  47.8 3.2 %collective-permute-done.2 = bf16[1,512,256]{2,1,0:T(8,128)(2,1)S(1)} collective-permute-done((bf16[1,512,256]{2,1,0:T(8,128)(2,1)S(1)}, bf16[1,512,256]{2,1,0:T(8,128)(2,1)S(1)}, u32[]{:S(2)}, u32[]{:S(2)}) %collective-permute-start.2) | collective-permute-done | bytes 262176 | tf_op jit(solution)/shard_map/ppermute | solution.py:708
  51.0 10.3 %all-to-all-done.inp = bf16[32,80,128]{2,1,0:T(8,128)(2,1)S(1)} async-done(((bf16[32,80,128]{2,1,0:T(8,128)(2,1)}), bf16[32,80,128]{2,1,0:T(8,128)(2,1)S(1)}, u32[]{:S(2)}, u32[]{:S(2)}) %all-to-all-start) | async-done | bytes 655392 | tf_op jit(solution)/shard_map/all_to_all | solution.py:701
  62.8 2.0 %near_stats.1.near = f32[8,512]{1,0:T(8,128)S(1)} custom-call(bf16[2,512,256]{2,1,0:T(8,128)(2,1)S(1)} %by_head.2.qo, bf16[2,512,256]{2,1,0:T(8,128)(2,1)} %by_head.3.kv), custom_call_target="tpu_custom_call" | custom-call | flops 268435456 | bytes 1048576 | tf_op jit(solution)/shard_map/near_stats/pallas_call | solution.py:154
  65.1 1.3 pad_add_fusion.listed
  66.4 1.5 pad_maximum_fusion.qos_in
  69.7 8.3 %all-to-all-start.1 = ((bf16[32,64,128]{2,1,0:T(8,128)(2,1)}), bf16[32,64,128]{2,1,0:T(8,128)(2,1)}, u32[]{:S(2)}, u32[]{:S(2)}) async-start(bf16[32,64,128]{2,1,0:T(8,128)(2,1)} %copy-done.1), calls=%async_computation.1 | async-start | bytes 1048576 | tf_op jit(solution)/shard_map/all_to_all | solution.py:701
  78.0 5.3 %all-gather.3.cloned.1.call-done = bf16[16,512,256]{2,1,0:T(8,128)(2,1)} async-done(((bf16[2,512,256]{2,1,0:T(8,128)(2,1)}), bf16[16,512,256]{2,1,0:T(8,128)(2,1)}) %all-gather.3.cloned.1.call-update) | async-done | bytes 4194320 | tf_op jit(solution)/shard_map/all_gather | solution.py:718
  84.1 5.0 %far_stats.1 = f32[5,8,512]{2,1,0:T(8,128)S(1)} custom-call(s32[137]{0:T(256)S(1)} %copy-done.7, f32[8,512]{1,0:T(8,128)S(1)} %near_stats.1.near, bf16[8,2,512,256]{3,2,1,0:T(8,128)(2,1)} %bitcast.23, bf16[4,2,512,256]{3,2,1,0:T(8,128)(2,1)S(1)} %pad_maximum_fusion.qos_in), custom_call_target="tpu_custom_call" | custom-call | flops 268435456 | bytes 6291456 | tf_op jit(solution)/shard_map/far_stats/pallas_call | solution.py:241
  89.1 1.8 %collective-permute-start.6 = (f32[5,8,512]{2,1,0:T(8,128)S(1)}, f32[5,8,512]{2,1,0:T(8,128)S(1)}, u32[]{:S(2)}, u32[]{:S(2)}) collective-permute-start(f32[5,8,512]{2,1,0:T(8,128)S(1)} %far_stats.1), channel_id=1, source_target_pairs={{0,192},{8,200},{16,208},{24,216},{32,224},{40,232},{48,240},{56,2... | collective-permute-start | bytes 245768 | tf_op jit(solution)/shard_map/ppermute | solution.py:708
  90.9 1.2 collective-permute-start.5
  93.2 3.2 %collective-permute-done.5 = f32[5,8,512]{2,1,0:T(8,128)S(1)} collective-permute-done((f32[5,8,512]{2,1,0:T(8,128)S(1)}, f32[5,8,512]{2,1,0:T(8,128)S(1)}, u32[]{:S(2)}, u32[]{:S(2)}) %collective-permute-start.5) | collective-permute-done | bytes 81952 | tf_op jit(solution)/shard_map/ppermute | solution.py:708
  96.4 1.2 collective-permute-done.4
  97.7 9.5 %far_grads.1 = (bf16[8,1024,256]{2,1,0:T(8,128)(2,1)}, bf16[68,128,256]{2,1,0:T(8,128)(2,1)}) custom-call(s32[137]{0:T(256)S(1)} %copy-done.7, s32[1]{0:T(128)} %bitcast.me, f32[4,5,8,512]{3,2,1,0:T(8,128)S(1)} %pad_maximum_fusion.1.stats, bf16[8,2,512,256]{3,2,1,0:T(8,128)(2,1)} %bitcast.24, bf16[4,2,512,256]{3,2,1,0:T(8,128)(2,1)S(1)} %pad_maximum_fusion.qos_in), custom_call_target="tpu_custom_call" | custom-call | flops 536870912 | bytes 12582912 | tf_op jit(solution)/shard_map/far_grads/pallas_call | solution.py:337
  107.2 1.2 copy-done.10
  110.5 1.6 copy-done.18
  112.1 12.8 %scan_grads.1 = (bf16[512,1024]{1,0:T(8,128)(2,1)}, f32[512,16]{1,0:T(8,128)S(1)}, bf16[1024,128]{1,0:T(8,128)(2,1)}) custom-call(bf16[512,1024]{1,0:T(8,128)(2,1)S(1)} %copy-done.10, bf16[512,1024]{1,0:T(8,128)(2,1)S(1)} %copy-done.12, f32[512,16]{1,0:T(8,128)S(1)} %copy.31.ld_ref, bf16[512,128]{1,0:T(8,128)(2,1)S(1)} %copy-done.14, ...), custom_call_target="tpu_custom_call" | custom-call | flops 4294967296 | bytes 12582912 | tf_op jit(solution)/shard_map/scan_grads/pallas_call | solution.py:680
  124.9 6.1 %all-to-all-start.3 = ((bf16[8,128,128]{2,1,0:T(8,128)(2,1)}), bf16[8,128,128]{2,1,0:T(8,128)(2,1)S(1)}, u32[]{:S(2)}, u32[]{:S(2)}) async-start(bf16[8,128,128]{2,1,0:T(8,128)(2,1)} %bitcast.20), calls=%async_computation.4 | async-start | bytes 524288 | tf_op jit(solution)/shard_map/all_to_all | solution.py:739
  131.0 2.2 %copy-done = bf16[16,512,256]{2,1,0:T(8,128)(2,1)S(1)} copy-done((bf16[16,512,256]{2,1,0:T(8,128)(2,1)S(1)}, bf16[16,512,256]{2,1,0:T(8,128)(2,1)}, u32[]{:S(2)}) %copy-start) | copy-done | bytes 4194328
  133.2 4.1 %far_queries.1 = bf16[4,512,256]{2,1,0:T(8,128)(2,1)} custom-call(s32[137]{0:T(256)S(1)} %copy-done.8, s32[1]{0:T(128)} %bitcast.me, bf16[68,128,256]{2,1,0:T(8,128)(2,1)} %get-tuple-element.33.ds_in, bf16[8,2,512,256]{3,2,1,0:T(8,128)(2,1)S(1)} %bitcast.25), custom_call_target="tpu_custom_call" | custom-call | flops 134217728 | bytes 6291456 | tf_op jit(solution)/shard_map/far_queries/pallas_call | solution.py:398
  137.5 3.5 %all-to-all-start.2 = ((bf16[4,512,256]{2,1,0:T(8,128)(2,1)}), bf16[4,512,256]{2,1,0:T(8,128)(2,1)S(1)}, u32[]{:S(2)}, u32[]{:S(2)}) async-start(bf16[4,512,256]{2,1,0:T(8,128)(2,1)} %far_queries.1), calls=%async_computation.2 | async-start | bytes 2097152 | tf_op jit(solution)/shard_map/all_to_all | solution.py:701
  141.8 13.7 %all_gather.11 = bf16[1024,128]{1,0:T(8,128)(2,1)S(1)} all-gather(bf16[128,128]{1,0:T(8,128)(2,1)S(1)} %reduce_sum.52), channel_id=1, replica_groups=mesh['seq'=32,'head'=8] {'head'}, dimensions={0}, use_global_device_ids=true | all-gather | bytes 294912 | tf_op jit(solution)/shard_map/all_gather | solution.py:742
  156.3 4.5 %near_grads.1 = (bf16[1024,128]{1,0:T(8,128)(2,1)}, f32[2,512,256]{2,1,0:T(8,128)S(1)}) custom-call(s32[1]{0:T(128)} %bitcast.me, f32[4,5,8,512]{3,2,1,0:T(8,128)S(1)} %pad_maximum_fusion.1.stats, bf16[2,512,256]{2,1,0:T(8,128)(2,1)S(1)} %by_head.2.qo, bf16[2,512,256]{2,1,0:T(8,128)(2,1)} %by_head.3.kv, bf16[4,512,256]{2,1,0:T(8,128)(2,1)S(1)} %all-to-all-done.2.dq_far), custom_call_target="tpu_custom_call" | custom-call | flops 671088640 | bytes 4194304 | tf_op jit(solution)/shard_map/near_grads/pallas_call | solution.py:445
  160.8 1.7 reduce-scatter.2.cloned.1.call-done
  (79 shorter events, 18.6 us)
Async XLA Ops:
  7.2 76.2 %all-gather.3.cloned.1.call-start = ((), (), s32[]{:S(2)}) async-start(), calls=%async_computation.6 | async-start | bytes 4718592 | tf_op jit(solution)/shard_map/all_gather | solution.py:718
  7.2 1.0 copy-start.3
  8.2 0.9 copy-start.4
  9.1 6.4 %copy-start.19 = (f32[512,16]{0,1:T(8,128)S(1)}, f32[512,16]{0,1:T(8,128)}, u32[]{:S(2)}) copy-start(f32[512,16]{0,1:T(8,128)} %param.17) | copy-start | bytes 98308
  9.1 6.6 %copy-start.9 = (bf16[512,1024]{1,0:T(8,128)(2,1)S(1)}, bf16[512,1024]{1,0:T(8,128)(2,1)}, u32[]{:S(2)}) copy-start(bf16[512,1024]{1,0:T(8,128)(2,1)} %x_ref.3) | copy-start | bytes 3145732
  9.1 6.6 %copy-start.13 = (bf16[512,128]{1,0:T(8,128)(2,1)S(1)}, bf16[512,128]{1,0:T(8,128)(2,1)}, u32[]{:S(2)}) copy-start(bf16[512,128]{1,0:T(8,128)(2,1)} %b_ref.3) | copy-start | bytes 393220
  9.1 6.6 %copy-start.15 = (bf16[512,128]{1,0:T(8,128)(2,1)S(1)}, bf16[512,128]{1,0:T(8,128)(2,1)}, u32[]{:S(2)}) copy-start(bf16[512,128]{1,0:T(8,128)(2,1)} %c_ref.3) | copy-start | bytes 393220
  10.1 1.0 copy-start.5
  11.1 0.9 copy-start.6
  12.2 14.0 %collective-permute-start.1 = (bf16[2,512,256]{2,1,0:T(8,128)(2,1)S(1)}, bf16[2,512,256]{2,1,0:T(8,128)(2,1)}, u32[]{:S(2)}, u32[]{:S(2)}) collective-permute-start(bf16[2,512,256]{2,1,0:T(8,128)(2,1)S(1)} %by_head.2.qo), channel_id=1, source_target_pairs={{0,192},{8,200},{16,208},{24,216},{32,224},{40,232},{48,240},{56,2... | collective-permute-start | bytes 1572872 | tf_op jit(solution)/shard_map/ppermute | solution.py:708
  15.5 13.8 %collective-permute-start = (bf16[2,512,256]{2,1,0:T(8,128)(2,1)S(1)}, bf16[2,512,256]{2,1,0:T(8,128)(2,1)}, u32[]{:S(2)}, u32[]{:S(2)}) collective-permute-start(bf16[2,512,256]{2,1,0:T(8,128)(2,1)S(1)} %by_head.2.qo), channel_id=1, source_target_pairs={{0,64},{8,72},{16,80},{24,88},{32,96},{40,104},{48,112},{56,120},{... | collective-permute-start | bytes 1572872 | tf_op jit(solution)/shard_map/ppermute | solution.py:708
  15.7 1.2 copy-start.11
  16.9 21.0 %copy-start.20 = (s32[128,4]{0,1:T(4,128)S(1)}, s32[128,4]{0,1:T(4,128)}, u32[]{:S(2)}) copy-start(s32[128,4]{0,1:T(4,128)} %param.22) | copy-start | bytes 6148
  16.9 21.1 %copy-start.21 = (s32[128,4]{0,1:T(4,128)S(1)}, s32[128,4]{0,1:T(4,128)}, u32[]{:S(2)}) copy-start(s32[128,4]{0,1:T(4,128)} %param.21) | copy-start | bytes 6148
  16.9 21.1 %copy-start.22 = (s32[128]{0:T(128)S(1)}, s32[128]{0:T(128)}, u32[]{:S(2)}) copy-start(s32[128]{0:T(128)} %param.23) | copy-start | bytes 1540
  21.5 1.3 copy-start.17
  29.3 32.0 %all-to-all-start = ((bf16[32,80,128]{2,1,0:T(8,128)(2,1)}), bf16[32,80,128]{2,1,0:T(8,128)(2,1)S(1)}, u32[]{:S(2)}, u32[]{:S(2)}) async-start(bf16[32,80,128]{2,1,0:T(8,128)(2,1)} %get-tuple-element.28), calls=%async_computation | async-start | bytes 1310720 | tf_op jit(solution)/shard_map/all_to_all | solution.py:701
  39.0 8.8 %collective-permute-start.3 = (bf16[1,512,256]{2,1,0:T(8,128)(2,1)S(1)}, bf16[1,512,256]{2,1,0:T(8,128)(2,1)S(1)}, u32[]{:S(2)}, u32[]{:S(2)}) collective-permute-start(bf16[1,512,256]{2,1,0:T(8,128)(2,1)S(1)} %slice.19), channel_id=1, source_target_pairs={{0,192},{8,200},{16,208},{24,216},{32,224},{40,232},{48,240},{56,2... | collective-permute-start | bytes 786440 | tf_op jit(solution)/shard_map/ppermute | solution.py:708
  42.5 8.5 %collective-permute-start.2 = (bf16[1,512,256]{2,1,0:T(8,128)(2,1)S(1)}, bf16[1,512,256]{2,1,0:T(8,128)(2,1)S(1)}, u32[]{:S(2)}, u32[]{:S(2)}) collective-permute-start(bf16[1,512,256]{2,1,0:T(8,128)(2,1)S(1)} %slice.18), channel_id=1, source_target_pairs={{0,64},{8,72},{16,80},{24,88},{32,96},{40,104},{48,112},{56,120},{... | collective-permute-start | bytes 786440 | tf_op jit(solution)/shard_map/ppermute | solution.py:708
  69.7 37.5 %all-to-all-start.1 = ((bf16[32,64,128]{2,1,0:T(8,128)(2,1)}), bf16[32,64,128]{2,1,0:T(8,128)(2,1)}, u32[]{:S(2)}, u32[]{:S(2)}) async-start(bf16[32,64,128]{2,1,0:T(8,128)(2,1)} %copy-done.1), calls=%async_computation.1 | async-start | bytes 1048576 | tf_op jit(solution)/shard_map/all_to_all | solution.py:701
  78.0 84.5 %reduce-scatter.2.cloned.1.call-start = ((), (), s32[]{:S(2)}) async-start(), calls=%async_computation.5 | async-start | bytes 4718592 | tf_op jit(solution)/shard_map/reduce_scatter | solution.py:734
  89.1 4.1 %collective-permute-start.6 = (f32[5,8,512]{2,1,0:T(8,128)S(1)}, f32[5,8,512]{2,1,0:T(8,128)S(1)}, u32[]{:S(2)}, u32[]{:S(2)}) collective-permute-start(f32[5,8,512]{2,1,0:T(8,128)S(1)} %far_stats.1), channel_id=1, source_target_pairs={{0,192},{8,200},{16,208},{24,216},{32,224},{40,232},{48,240},{56,2... | collective-permute-start | bytes 245768 | tf_op jit(solution)/shard_map/ppermute | solution.py:708
  90.9 5.5 %collective-permute-start.5 = (f32[5,8,512]{2,1,0:T(8,128)S(1)}, f32[5,8,512]{2,1,0:T(8,128)S(1)}, u32[]{:S(2)}, u32[]{:S(2)}) collective-permute-start(f32[5,8,512]{2,1,0:T(8,128)S(1)} %far_stats.1), channel_id=1, source_target_pairs={{0,128},{8,136},{16,144},{24,152},{32,160},{40,168},{48,176},{56,1... | collective-permute-start | bytes 245768 | tf_op jit(solution)/shard_map/ppermute | solution.py:708
  92.1 5.5 %collective-permute-start.4 = (f32[5,8,512]{2,1,0:T(8,128)S(1)}, f32[5,8,512]{2,1,0:T(8,128)S(1)}, u32[]{:S(2)}, u32[]{:S(2)}) collective-permute-start(f32[5,8,512]{2,1,0:T(8,128)S(1)} %far_stats.1), channel_id=1, source_target_pairs={{0,64},{8,72},{16,80},{24,88},{32,96},{40,104},{48,112},{56,120},{... | collective-permute-start | bytes 245768 | tf_op jit(solution)/shard_map/ppermute | solution.py:708
  107.1 1.2 copy-start.10
  107.2 1.5 copy-start.12
  110.5 1.6 copy-start.18
  112.1 18.9 %copy-start.8 = (s32[137]{0:T(256)S(1)}, s32[137]{0:T(256)}, u32[]{:S(2)}) copy-start(s32[137]{0:T(256)} %pad_add_fusion.listed) | copy-start | bytes 1648
  124.9 12.6 %all-to-all-start.3 = ((bf16[8,128,128]{2,1,0:T(8,128)(2,1)}), bf16[8,128,128]{2,1,0:T(8,128)(2,1)S(1)}, u32[]{:S(2)}, u32[]{:S(2)}) async-start(bf16[8,128,128]{2,1,0:T(8,128)(2,1)} %bitcast.20), calls=%async_computation.4 | async-start | bytes 524288 | tf_op jit(solution)/shard_map/all_to_all | solution.py:739
  131.0 2.2 %copy-start = (bf16[16,512,256]{2,1,0:T(8,128)(2,1)S(1)}, bf16[16,512,256]{2,1,0:T(8,128)(2,1)}, u32[]{:S(2)}) copy-start(bf16[16,512,256]{2,1,0:T(8,128)(2,1)} %all-gather.3.cloned.1.call-done) | copy-start | bytes 12582916
  137.5 18.8 %all-to-all-start.2 = ((bf16[4,512,256]{2,1,0:T(8,128)(2,1)}), bf16[4,512,256]{2,1,0:T(8,128)(2,1)S(1)}, u32[]{:S(2)}, u32[]{:S(2)}) async-start(bf16[4,512,256]{2,1,0:T(8,128)(2,1)} %far_queries.1), calls=%async_computation.2 | async-start | bytes 2097152 | tf_op jit(solution)/shard_map/all_to_all | solution.py:701
  162.5 1.0 copy-start.2
  (4 other events, 3.3 us)
Sparse Core Ops, SparseCore 0:
  10.2 73.1 all-gather.2
  107.3 55.0 reduce-scatter.1

commit v3 on v2

--- a/solution.py
+++ b/solution.py
@@ -182,71 +182,112 @@
     return wait
 
 
-def load_far(column_in, qos_in, column, qos, sems):
-    return load(
-        [(column_in.at[z], column.at[z]) for z in range(NZ)]
-        + [(qos_in.at[d], qos.at[d]) for d in range(NX)],
-        sems,
-    )
-
-
-def far_scratch():
-    return [
-        pltpu.VMEM((NZ, 2, TOK, PAIR), BF16),
-        pltpu.VMEM((NX, 2, TOK, PAIR), BF16),
-        pltpu.SemaphoreType.DMA((NZ + NX,)),
-    ]
-
-
-def fetch(qos, keys, place, block):
+TILES = NX * ITEMS + UNROLL
+
+
+def tile_copies(a, b, sems):
+    def group(t):
+        tiles = pl.ds(UNROLL * t, UNROLL)
+        return pltpu.make_async_copy(a.at[tiles], b.at[tiles], sems.at[t])
+
+    return group
+
+
+def tile_sems():
+    return pltpu.SemaphoreType.DMA((TILES // UNROLL,))
+
+
+def each(count, act):
+    def step(t, _):
+        act(t)
+        return 0
+
+    lax.fori_loop(0, count, step, 0)
+
+
+def queries(qos, block):
     n = jnp.minimum(block, NX * SEG - 1)
-    d = n >> 2
     rows = span(n & (SEG - 1))
-    z = place >> 2
-    cols = span(place & (SEG - 1))
-    return (
-        spread(qos[d, 0, rows, :]), spread(qos[d, 1, rows, :]), keys[z, 0, cols, :], keys[z, 1, cols, :]
-    )
-
-
-def far_stats_body(listed, near, column_in, qos_in, out, tally, column, qos, sems):
-    ready = load_far(column_in, qos_in, column, qos, sems)
+    return spread(qos[n >> 2, 0, rows, :]), spread(qos[n >> 2, 1, rows, :])
+
+
+def far_stats_body(
+    listed, near, column_in, qos, out, high_out, e_out, dp_out,
+    tally, column, e_keep, dp_keep, sems, e_sems, dp_sems,
+):
+    ready = load([(column_in.at[z], column.at[z]) for z in range(NZ)], sems)
     items = Listed(listed)
+    e_sent = tile_copies(e_keep, e_out, e_sems)
+    dp_sent = tile_copies(dp_keep, dp_out, dp_sems)
     kind = lax.broadcasted_iota(jnp.int32, (4, PAIR), 0)
     start = jnp.where(kind == 0, EMPTY, 0.0)
     for n in range(NX * SEG + 1):
         tally[n] = start
     ready()
 
-    def visit(numbers):
-        found = [summary(*fetch(qos, column, items.place(n), items.block(n))) for n in numbers]
-        for n, (m, l, t) in zip(numbers, found):
+    def group(t):
+        numbers = [UNROLL * t + i for i in range(UNROLL)]
+        found = []
+        for n in numbers:
+            place = items.place(n)
+            cols = span(place & (SEG - 1))
+            q, o = queries(qos, items.block(n))
+            s = mm_nt(column[place >> 2, 0, cols, :], q) * SCALE
+            dp = mm_nt(column[place >> 2, 1, cols, :], o)
+            m = jnp.max(s, axis=0, keepdims=True)
+            e = jnp.exp(s - m)
+            found.append(
+                (m, jnp.sum(e, axis=0, keepdims=True), jnp.sum(e * dp, axis=0, keepdims=True))
+            )
+            e_keep[n] = e.astype(BF16)
+            dp_keep[n] = dp.astype(BF16)
+            high_out[n] = jnp.broadcast_to(m, (8, PAIR))
+        e_sent(t).start()
+        dp_sent(t).start()
+        for n, (m, l, t_sum) in zip(numbers, found):
             old = tally[items.block(n)]
             m0, l0, t0 = [old[i : i + 1, :] for i in range(KINDS)]
             high = jnp.maximum(m0, m)
             f0 = jnp.exp(m0 - high)
             f1 = jnp.exp(m - high)
             tally[items.block(n)] = jnp.concatenate(
-                [high, l0 * f0 + l * f1, t0 * f0 + t * f1, jnp.zeros_like(high)], axis=0
+                [high, l0 * f0 + l * f1, t0 * f0 + t_sum * f1, jnp.zeros_like(high)], axis=0
             )
 
-    in_groups(items.count, visit)
+    groups = (items.count + UNROLL - 1) // UNROLL
+    each(groups, group)
     for d in range(NX):
         out[d] = packed([tally[d * SEG + b] for b in range(SEG)])
     out[NX] = near[...]
+    each(groups, lambda t: e_sent(t).wait())
+    each(groups, lambda t: dp_sent(t).wait())
 
 
 def far_stats(listed, near, column, qos):
     vm = pltpu.VMEM
+    tiles = (TILES, BLK, PAIR)
     return call(
         far_stats_body,
         "far_stats",
-        [((NX + 1, 8, 2 * PAIR), F32, vm)],
-        [pltpu.SMEM, vm, pltpu.HBM, pl.ANY],
-        [vm((NX * SEG + 1, 4, PAIR), F32)] + far_scratch(),
+        [
+            ((NX + 1, 8, 2 * PAIR), F32, vm),
+            ((TILES, 8, PAIR), F32, vm),
+            (tiles, BF16, pltpu.HBM),
+            (tiles, BF16, pltpu.HBM),
+        ],
+        [pltpu.SMEM, vm, pltpu.HBM, vm],
+        [
+            vm((NX * SEG + 1, 4, PAIR), F32),
+            vm((NZ, 2, TOK, PAIR), BF16),
+            vm(tiles, BF16),
+            vm(tiles, BF16),
+            pltpu.SemaphoreType.DMA((NZ,)),
+            tile_sems(),
+            tile_sems(),
+        ],
         2 * 2 * 2 * 16 * BLK * BLK * HD,
         6 << 20,
-    )(listed, near, column, qos)[0]
+    )(listed, near, column, qos)
 
 
 def joined(stats, my_x, x_q):
@@ -273,47 +314,49 @@
     return p.astype(BF16), ds
 
 
-def ds_copies(a, b, sems):
-    def group(t):
-        tiles = pl.ds(UNROLL * t, UNROLL)
-        return pltpu.make_async_copy(a.at[tiles], b.at[tiles], sems.at[t])
-
-    return group
-
-
 def far_grads_body(
-    listed, me, stats, column_in, qos_in, kv_out, ds_out,
-    total, rowed, staged, ds_keep, column, qos, sems, out_sems, ds_sems,
+    listed, me, stats, highs, e_in, dp_in, qos, kv_out, ds_out,
+    total, rowed, staged, ds_keep, e_keep, dp_keep, out_sems, ds_sems, e_sems, dp_sems,
 ):
-    ready = load_far(column_in, qos_in, column, qos, sems)
     my_x = me[0] >> 3
     items = Listed(listed)
-    sent = ds_copies(ds_keep, ds_out, ds_sems)
+    groups = (items.count + UNROLL - 1) // UNROLL
+    sent = tile_copies(ds_keep, ds_out, ds_sems)
+    e_got = tile_copies(e_in, e_keep, e_sems)
+    dp_got = tile_copies(dp_in, dp_keep, dp_sems)
+
+    def begin(t):
+        e_got(t).start()
+        dp_got(t).start()
+
+    each(groups, begin)
     total[...] = jnp.zeros_like(total)
     for d in range(NX):
         tile = joined(stats, my_x, (my_x - d) & (NX - 1))
         for b in range(SEG):
             rowed[d * SEG + b, 0:KINDS, :] = unpacked(tile, b)
     rowed[NX * SEG] = jnp.zeros((8, PAIR), F32)
-    ready()
-
-    def group(t, _):
+
+    def group(t):
+        e_got(t).wait()
+        dp_got(t).wait()
         numbers = [UNROLL * t + i for i in range(UNROLL)]
         found = []
         for n in numbers:
-            q, o, k, v = fetch(qos, column, items.place(n), items.block(n))
-            p, ds = weights_of(q, o, k, v, rowed[items.block(n)])
-            found.append((ds, mm(ds, q), mm(p, o)))
+            row = rowed[items.block(n)]
+            high, inverse, delta = [row[i : i + 1, :] for i in range(KINDS)]
+            q, o = queries(qos, items.block(n))
+            p = e_keep[n].astype(F32) * (jnp.exp(highs[n][0:1, :] - high) * inverse)
+            ds = (p * (dp_keep[n].astype(F32) - delta) * SCALE).astype(BF16)
+            found.append((ds, mm(ds, q), mm(p.astype(BF16), o)))
         for n, (ds, dk, dv) in zip(numbers, found):
             to = jnp.where(items.block(n) == NX * SEG, FAR, items.place(n))
             ds_keep[n] = ds
             total[to, 0] += dk
             total[to, 1] += dv
         sent(t).start()
-        return 0
-
-    groups = (items.count + UNROLL - 1) // UNROLL
-    lax.fori_loop(0, groups, group, 0)
+
+    each(groups, group)
     copies = []
     for z in range(NZ):
         for s in range(2):
@@ -321,45 +364,41 @@
                 staged[z, pl.ds(s * TOK + b * BLK, BLK), :] = total[z * SEG + b, s].astype(BF16)
         copies.append(pltpu.make_async_copy(staged.at[z], kv_out.at[z], out_sems.at[z]))
         copies[-1].start()
-
-    def drain(t, _):
-        sent(t).wait()
-        return 0
-
-    lax.fori_loop(0, groups, drain, 0)
+    each(groups, lambda t: sent(t).wait())
     for copy in copies:
         copy.wait()
 
 
-def far_grads(listed, me, stats, column, qos):
-    vm = pltpu.VMEM
-    tiles = NX * ITEMS + UNROLL
+def far_grads(listed, me, stats, highs, e, dp, qos):
+    vm = pltpu.VMEM
+    tiles = (TILES, BLK, PAIR)
     return call(
         far_grads_body,
         "far_grads",
-        [
-            ((NZ, 2 * TOK, PAIR), BF16, pltpu.HBM),
-            ((tiles, BLK, PAIR), BF16, pltpu.HBM),
-        ],
-        [pltpu.SMEM, pltpu.SMEM, vm, pltpu.HBM, pl.ANY],
+        [((NZ, 2 * TOK, PAIR), BF16, pltpu.HBM), (tiles, BF16, pltpu.HBM)],
+        [pltpu.SMEM, pltpu.SMEM, vm, vm, pltpu.HBM, pltpu.HBM, vm],
         [
             vm((FAR + 1, 2, BLK, PAIR), F32),
             vm((NX * SEG + 1, 8, PAIR), F32),
             vm((NZ, 2 * TOK, PAIR), BF16),
-            vm((tiles, BLK, PAIR), BF16),
-        ]
-        + far_scratch()
-        + [pltpu.SemaphoreType.DMA((NZ,)), pltpu.SemaphoreType.DMA((tiles // UNROLL,))],
+            vm(tiles, BF16),
+            vm(tiles, BF16),
+            vm(tiles, BF16),
+            pltpu.SemaphoreType.DMA((NZ,)),
+            tile_sems(),
+            tile_sems(),
+            tile_sems(),
+        ],
         4 * 2 * 2 * 16 * BLK * BLK * HD,
         12 << 20,
-    )(listed, me, stats, column, qos)
+    )(listed, me, stats, highs, e, dp, qos)
 
 
 def far_queries_body(listed, me, ds_in, column_in, dq_out, dq, ds_keep, keys, sems, ds_sems):
     ready = load([(column_in.at[z, 0], keys.at[z]) for z in range(NZ)], sems)
     my_x = me[0] >> 3
     items = Listed(listed)
-    fetched = ds_copies(ds_in, ds_keep, ds_sems)
+    fetched = tile_copies(ds_in, ds_keep, ds_sems)
     groups = (items.count + UNROLL - 1) // UNROLL
 
     def begin(t, _):
@@ -728,9 +767,9 @@
     qos = jnp.stack([qo, shifted[0], opposite, shifted[1]])
     near = near_stats(after(qo, pay), kv)
     carried = exchange(scan_prefix(after(pay, near, listed, qos)))
-    stats = far_stats(listed, near, column, qos)
+    stats, highs, e_far, dp_far = far_stats(listed, near, column, qos)
     stats = jnp.stack([stats] + [along_x(stats, d) for d in range(1, NX)])
-    kv_far, ds_far = far_grads(listed, me, stats, column, qos)
+    kv_far, ds_far = far_grads(listed, me, stats, highs, e_far, dp_far, qos)
     kv_far = lax.psum_scatter(
         after(kv_far, carried), "seq", scatter_dimension=0, axis_index_groups=Z_GROUPS
     )

time: 173 us -> 169 us (0.977)
  Pallas kernels: 45.4 us -> 42.5 us
    pallas_call x1, Pallas kernels: 9.45 us -> 5.64 us  [far_grads(): call(far_grads_body, 'far_grads', [((NZ, 2 * TOK, PAIR), BF16, pltpu.HBM)...]
  transfers between devices with their start and end apart: 13 -> 13, of which waited for: 11 -> 11; matrix products, arithmetic and copies ran while one was open for 5% -> 5% of each run, Pallas kernels for 25% -> 24%
where the time goes in v3:
time: 169 us; the launch traced here: 168 us
  Pallas kernels  42.5 us (25%)
  starting transfers between devices  36.8 us (22%)
  waiting for transfers between devices  36 us (21%)
  local copies, waits for them, and re-layouts  20.7 us (12%)
  between operations  14.3 us (8%)
  blocking collectives  13.7 us (8%)
  other arithmetic  3.85 us (2%)
    all_to_all x3, starting transfers between devices, exchange(): lax.all_to_all(value, 'seq', 0, 0, tiled=True, axis_index_groups=groups)  20.4 us
    ppermute x7, waiting for transfers between devices, along_x(): return lax.ppermute(value, 'seq', pairs)  19.2 us
    unnamed x48, local copies, waits for them, and re-layouts  16.9 us
    all_gather x1, blocking collectives, per_device(): whole = lax.all_gather(part, 'head', tiled=True).astype(F32)  13.7 us
    pallas_call x1, Pallas kernels, scan_grads(): call(grads_body, 'scan_grads', [((TOK, WIDTH), BF16, vm), ((TOK, SH), F32...  12.8 us
    all_to_all x3, waiting for transfers between devices, exchange(): lax.all_to_all(value, 'seq', 0, 0, tiled=True, axis_index_groups=groups)  10.3 us
    ppermute x7, starting transfers between devices, along_x(): return lax.ppermute(value, 'seq', pairs)  9.64 us
    all_to_all x1, starting transfers between devices, per_device(): shares = lax.all_to_all(bc.reshape(8, 128, NST), 'head', 0, 0, tiled=True)  6.64 us
  transfers between devices with their start and end apart: 13, of which 11 were waited for; matrix products, arithmetic and copies ran while one was open for 5% of the time, Pallas kernels for 24%

profile of v3, /device:TPU:1, one launch (start us, length us, event | category | flops | bytes accessed | tf_op | source)
XLA Modules:
  0.0 167.9 jit_solution(3790203082432331181)
XLA Ops:
  12.2 3.4 %collective-permute-start.1 = (bf16[2,512,256]{2,1,0:T(8,128)(2,1)S(1)}, bf16[2,512,256]{2,1,0:T(8,128)(2,1)}, u32[]{:S(2)}, u32[]{:S(2)}) collective-permute-start(bf16[2,512,256]{2,1,0:T(8,128)(2,1)S(1)} %by_head.2.qo), channel_id=1, source_target_pairs={{0,192},{8,200},{16,208},{24,216},{32,224},{40,232},{48,240},{56,2... | collective-permute-start | bytes 1572872 | tf_op jit(solution)/shard_map/ppermute | solution.py:747
  15.7 1.2 copy-done.11
  16.9 4.6 %scan_ends.1 = (f32[4,1024,128]{2,1,0:T(8,128)S(1)}, f32[4,1024,128]{2,1,0:T(8,128)}, bf16[32,80,128]{2,1,0:T(8,128)(2,1)}) custom-call(bf16[512,1024]{1,0:T(8,128)(2,1)S(1)} %copy-done.9, bf16[512,1024]{1,0:T(8,128)(2,1)S(1)} %copy-done.11, f32[512,16]{1,0:T(8,128)S(1)} %copy.31.ld_ref, bf16[512,128]{1,0:T(8,128)(2,1)S(1)} %copy-done.13, ...), custom_call_target="tpu_custom_call" | custom-call | flops 1073741824 | bytes 8388608 | tf_op jit(solution)/shard_map/scan_ends/pallas_call | solution.py:602
  21.5 1.4 copy-done.17
  22.9 3.2 %collective-permute-done.1 = bf16[2,512,256]{2,1,0:T(8,128)(2,1)} collective-permute-done((bf16[2,512,256]{2,1,0:T(8,128)(2,1)S(1)}, bf16[2,512,256]{2,1,0:T(8,128)(2,1)}, u32[]{:S(2)}, u32[]{:S(2)}) %collective-permute-start.1) | collective-permute-done | bytes 524320 | tf_op jit(solution)/shard_map/ppermute | solution.py:747
  26.1 3.2 %collective-permute-done = bf16[2,512,256]{2,1,0:T(8,128)(2,1)} collective-permute-done((bf16[2,512,256]{2,1,0:T(8,128)(2,1)S(1)}, bf16[2,512,256]{2,1,0:T(8,128)(2,1)}, u32[]{:S(2)}, u32[]{:S(2)}) %collective-permute-start) | collective-permute-done | bytes 524320 | tf_op jit(solution)/shard_map/ppermute | solution.py:747
  29.3 8.6 %all-to-all-start = ((bf16[32,80,128]{2,1,0:T(8,128)(2,1)}), bf16[32,80,128]{2,1,0:T(8,128)(2,1)S(1)}, u32[]{:S(2)}, u32[]{:S(2)}) async-start(bf16[32,80,128]{2,1,0:T(8,128)(2,1)} %get-tuple-element.32), calls=%async_computation | async-start | bytes 1310720 | tf_op jit(solution)/shard_map/all_to_all | solution.py:740
  38.0 1.0 slice.19
  39.0 2.6 %collective-permute-start.3 = (bf16[1,512,256]{2,1,0:T(8,128)(2,1)S(1)}, bf16[1,512,256]{2,1,0:T(8,128)(2,1)S(1)}, u32[]{:S(2)}, u32[]{:S(2)}) collective-permute-start(bf16[1,512,256]{2,1,0:T(8,128)(2,1)S(1)} %slice.19), channel_id=1, source_target_pairs={{0,192},{8,200},{16,208},{24,216},{32,224},{40,232},{48,240},{56,2... | collective-permute-start | bytes 786440 | tf_op jit(solution)/shard_map/ppermute | solution.py:747
  42.9 4.9 %collective-permute-done.3 = bf16[1,512,256]{2,1,0:T(8,128)(2,1)S(1)} collective-permute-done((bf16[1,512,256]{2,1,0:T(8,128)(2,1)S(1)}, bf16[1,512,256]{2,1,0:T(8,128)(2,1)S(1)}, u32[]{:S(2)}, u32[]{:S(2)}) %collective-permute-start.3) | collective-permute-done | bytes 262176 | tf_op jit(solution)/shard_map/ppermute | solution.py:747
  47.8 3.2 %collective-permute-done.2 = bf16[1,512,256]{2,1,0:T(8,128)(2,1)S(1)} collective-permute-done((bf16[1,512,256]{2,1,0:T(8,128)(2,1)S(1)}, bf16[1,512,256]{2,1,0:T(8,128)(2,1)S(1)}, u32[]{:S(2)}, u32[]{:S(2)}) %collective-permute-start.2) | collective-permute-done | bytes 262176 | tf_op jit(solution)/shard_map/ppermute | solution.py:747
  51.0 10.3 %all-to-all-done.inp = bf16[32,80,128]{2,1,0:T(8,128)(2,1)S(1)} async-done(((bf16[32,80,128]{2,1,0:T(8,128)(2,1)}), bf16[32,80,128]{2,1,0:T(8,128)(2,1)S(1)}, u32[]{:S(2)}, u32[]{:S(2)}) %all-to-all-start) | async-done | bytes 655392 | tf_op jit(solution)/shard_map/all_to_all | solution.py:740
  62.8 2.0 %near_stats.1.near = f32[8,512]{1,0:T(8,128)S(1)} custom-call(bf16[2,512,256]{2,1,0:T(8,128)(2,1)S(1)} %by_head.2.qo, bf16[2,512,256]{2,1,0:T(8,128)(2,1)} %by_head.3.kv), custom_call_target="tpu_custom_call" | custom-call | flops 268435456 | bytes 1048576 | tf_op jit(solution)/shard_map/near_stats/pallas_call | solution.py:154
  65.1 1.3 pad_add_fusion.listed
  66.4 1.5 pad_maximum_fusion.qos
  69.7 8.3 %all-to-all-start.1 = ((bf16[32,64,128]{2,1,0:T(8,128)(2,1)}), bf16[32,64,128]{2,1,0:T(8,128)(2,1)}, u32[]{:S(2)}, u32[]{:S(2)}) async-start(bf16[32,64,128]{2,1,0:T(8,128)(2,1)} %copy-done.1), calls=%async_computation.1 | async-start | bytes 1048576 | tf_op jit(solution)/shard_map/all_to_all | solution.py:740
  78.0 5.3 %all-gather.3.cloned.1.call-done = bf16[16,512,256]{2,1,0:T(8,128)(2,1)} async-done(((bf16[2,512,256]{2,1,0:T(8,128)(2,1)}), bf16[16,512,256]{2,1,0:T(8,128)(2,1)}) %all-gather.3.cloned.1.call-update) | async-done | bytes 4194320 | tf_op jit(solution)/shard_map/all_gather | solution.py:757
  84.1 6.0 %far_stats.1 = (f32[5,8,512]{2,1,0:T(8,128)S(1)}, f32[68,8,256]{2,1,0:T(8,128)S(1)}, bf16[68,128,256]{2,1,0:T(8,128)(2,1)}, bf16[68,128,256]{2,1,0:T(8,128)(2,1)}) custom-call(s32[137]{0:T(256)S(1)} %copy-done.7, f32[8,512]{1,0:T(8,128)S(1)} %near_stats.1.near, bf16[8,2,512,256]{3,2,1,0:T(8,128)(2,1)} %bitcast.23, ...), custom_call_target="tpu_custom_call" | custom-call | flops 268435456 | bytes 6291456 | tf_op jit(solution)/shard_map/far_stats/pallas_call | solution.py:269
  90.1 2.9 %collective-permute-start.6 = (f32[5,8,512]{2,1,0:T(8,128)S(1)}, f32[5,8,512]{2,1,0:T(8,128)S(1)}, u32[]{:S(2)}, u32[]{:S(2)}) collective-permute-start(f32[5,8,512]{2,1,0:T(8,128)S(1)} %get-tuple-element.37), channel_id=1, source_target_pairs={{0,192},{8,200},{16,208},{24,216},{32,224},{40,232},{48,240},{56,2... | collective-permute-start | bytes 245768 | tf_op jit(solution)/shard_map/ppermute | solution.py:747
  93.7 1.0 collective-permute-done.6
  94.7 3.1 %collective-permute-done.5 = f32[5,8,512]{2,1,0:T(8,128)S(1)} collective-permute-done((f32[5,8,512]{2,1,0:T(8,128)S(1)}, f32[5,8,512]{2,1,0:T(8,128)S(1)}, u32[]{:S(2)}, u32[]{:S(2)}) %collective-permute-start.5) | collective-permute-done | bytes 81952 | tf_op jit(solution)/shard_map/ppermute | solution.py:747
  98.4 5.6 %far_grads.1 = (bf16[8,1024,256]{2,1,0:T(8,128)(2,1)}, bf16[68,128,256]{2,1,0:T(8,128)(2,1)}) custom-call(s32[137]{0:T(256)S(1)} %copy-done.7, s32[1]{0:T(128)} %bitcast.me, f32[4,5,8,512]{3,2,1,0:T(8,128)S(1)} %pad_maximum_fusion.1.stats, f32[68,8,256]{2,1,0:T(8,128)S(1)} %get-tuple-element.38.highs, bf16[68,128,256]{2,1,0:T(8,128)(2,1)} %get-tuple-element.39.e_in, ...), custom_call_target="tpu_custom_call" | custom-call | flops 536870912 | bytes 12582912 | tf_op jit(solution)/shard_map/far_grads/pallas_call | solution.py:375
  104.1 1.2 copy-done.10
  107.4 1.6 copy-done.18
  109.0 12.8 %scan_grads.1 = (bf16[512,1024]{1,0:T(8,128)(2,1)}, f32[512,16]{1,0:T(8,128)S(1)}, bf16[1024,128]{1,0:T(8,128)(2,1)}) custom-call(bf16[512,1024]{1,0:T(8,128)(2,1)S(1)} %copy-done.10, bf16[512,1024]{1,0:T(8,128)(2,1)S(1)} %copy-done.12, f32[512,16]{1,0:T(8,128)S(1)} %copy.31.ld_ref, bf16[512,128]{1,0:T(8,128)(2,1)S(1)} %copy-done.14, ...), custom_call_target="tpu_custom_call" | custom-call | flops 4294967296 | bytes 12582912 | tf_op jit(solution)/shard_map/scan_grads/pallas_call | solution.py:719
  121.8 6.6 %all-to-all-start.3 = ((bf16[8,128,128]{2,1,0:T(8,128)(2,1)}), bf16[8,128,128]{2,1,0:T(8,128)(2,1)S(1)}, u32[]{:S(2)}, u32[]{:S(2)}) async-start(bf16[8,128,128]{2,1,0:T(8,128)(2,1)} %bitcast.20), calls=%async_computation.4 | async-start | bytes 524288 | tf_op jit(solution)/shard_map/all_to_all | solution.py:778
  128.5 2.2 %copy-done = bf16[16,512,256]{2,1,0:T(8,128)(2,1)S(1)} copy-done((bf16[16,512,256]{2,1,0:T(8,128)(2,1)S(1)}, bf16[16,512,256]{2,1,0:T(8,128)(2,1)}, u32[]{:S(2)}) %copy-start) | copy-done | bytes 4194328
  130.7 4.1 %far_queries.1 = bf16[4,512,256]{2,1,0:T(8,128)(2,1)} custom-call(s32[137]{0:T(256)S(1)} %copy-done.8, s32[1]{0:T(128)} %bitcast.me, bf16[68,128,256]{2,1,0:T(8,128)(2,1)} %get-tuple-element.41.ds_in, bf16[8,2,512,256]{3,2,1,0:T(8,128)(2,1)S(1)} %bitcast.24), custom_call_target="tpu_custom_call" | custom-call | flops 134217728 | bytes 6291456 | tf_op jit(solution)/shard_map/far_queries/pallas_call | solution.py:437
  135.0 3.5 %all-to-all-start.2 = ((bf16[4,512,256]{2,1,0:T(8,128)(2,1)}), bf16[4,512,256]{2,1,0:T(8,128)(2,1)S(1)}, u32[]{:S(2)}, u32[]{:S(2)}) async-start(bf16[4,512,256]{2,1,0:T(8,128)(2,1)} %far_queries.1), calls=%async_computation.2 | async-start | bytes 2097152 | tf_op jit(solution)/shard_map/all_to_all | solution.py:740
  139.3 13.7 %all_gather.11 = bf16[1024,128]{1,0:T(8,128)(2,1)S(1)} all-gather(bf16[128,128]{1,0:T(8,128)(2,1)S(1)} %reduce_sum.52), channel_id=1, replica_groups=mesh['seq'=32,'head'=8] {'head'}, dimensions={0}, use_global_device_ids=true | all-gather | bytes 294912 | tf_op jit(solution)/shard_map/all_gather | solution.py:781
  153.8 4.5 %near_grads.1 = (bf16[1024,128]{1,0:T(8,128)(2,1)}, f32[2,512,256]{2,1,0:T(8,128)S(1)}) custom-call(s32[1]{0:T(128)} %bitcast.me, f32[4,5,8,512]{3,2,1,0:T(8,128)S(1)} %pad_maximum_fusion.1.stats, bf16[2,512,256]{2,1,0:T(8,128)(2,1)S(1)} %by_head.2.qo, bf16[2,512,256]{2,1,0:T(8,128)(2,1)} %by_head.3.kv, bf16[4,512,256]{2,1,0:T(8,128)(2,1)S(1)} %all-to-all-done.2.dq_far), custom_call_target="tpu_custom_call" | custom-call | flops 671088640 | bytes 4194304 | tf_op jit(solution)/shard_map/near_grads/pallas_call | solution.py:484
  159.2 1.0 copy-done.2
  (79 shorter events, 17.6 us)
Async XLA Ops:
  7.2 76.2 %all-gather.3.cloned.1.call-start = ((), (), s32[]{:S(2)}) async-start(), calls=%async_computation.6 | async-start | bytes 4718592 | tf_op jit(solution)/shard_map/all_gather | solution.py:757
  7.2 1.0 copy-start.3
  8.2 0.9 copy-start.4
  9.1 6.4 %copy-start.19 = (f32[512,16]{0,1:T(8,128)S(1)}, f32[512,16]{0,1:T(8,128)}, u32[]{:S(2)}) copy-start(f32[512,16]{0,1:T(8,128)} %param.17) | copy-start | bytes 98308
  9.1 6.6 %copy-start.9 = (bf16[512,1024]{1,0:T(8,128)(2,1)S(1)}, bf16[512,1024]{1,0:T(8,128)(2,1)}, u32[]{:S(2)}) copy-start(bf16[512,1024]{1,0:T(8,128)(2,1)} %x_ref.3) | copy-start | bytes 3145732
  9.1 6.6 %copy-start.13 = (bf16[512,128]{1,0:T(8,128)(2,1)S(1)}, bf16[512,128]{1,0:T(8,128)(2,1)}, u32[]{:S(2)}) copy-start(bf16[512,128]{1,0:T(8,128)(2,1)} %b_ref.3) | copy-start | bytes 393220
  9.1 6.6 %copy-start.15 = (bf16[512,128]{1,0:T(8,128)(2,1)S(1)}, bf16[512,128]{1,0:T(8,128)(2,1)}, u32[]{:S(2)}) copy-start(bf16[512,128]{1,0:T(8,128)(2,1)} %c_ref.3) | copy-start | bytes 393220
  10.1 1.0 copy-start.5
  11.1 0.9 copy-start.6
  12.2 14.0 %collective-permute-start.1 = (bf16[2,512,256]{2,1,0:T(8,128)(2,1)S(1)}, bf16[2,512,256]{2,1,0:T(8,128)(2,1)}, u32[]{:S(2)}, u32[]{:S(2)}) collective-permute-start(bf16[2,512,256]{2,1,0:T(8,128)(2,1)S(1)} %by_head.2.qo), channel_id=1, source_target_pairs={{0,192},{8,200},{16,208},{24,216},{32,224},{40,232},{48,240},{56,2... | collective-permute-start | bytes 1572872 | tf_op jit(solution)/shard_map/ppermute | solution.py:747
  15.5 13.8 %collective-permute-start = (bf16[2,512,256]{2,1,0:T(8,128)(2,1)S(1)}, bf16[2,512,256]{2,1,0:T(8,128)(2,1)}, u32[]{:S(2)}, u32[]{:S(2)}) collective-permute-start(bf16[2,512,256]{2,1,0:T(8,128)(2,1)S(1)} %by_head.2.qo), channel_id=1, source_target_pairs={{0,64},{8,72},{16,80},{24,88},{32,96},{40,104},{48,112},{56,120},{... | collective-permute-start | bytes 1572872 | tf_op jit(solution)/shard_map/ppermute | solution.py:747
  15.7 1.2 copy-start.11
  16.9 21.0 %copy-start.20 = (s32[128,4]{0,1:T(4,128)S(1)}, s32[128,4]{0,1:T(4,128)}, u32[]{:S(2)}) copy-start(s32[128,4]{0,1:T(4,128)} %param.22) | copy-start | bytes 6148
  16.9 21.1 %copy-start.21 = (s32[128,4]{0,1:T(4,128)S(1)}, s32[128,4]{0,1:T(4,128)}, u32[]{:S(2)}) copy-start(s32[128,4]{0,1:T(4,128)} %param.21) | copy-start | bytes 6148
  16.9 21.1 %copy-start.22 = (s32[128]{0:T(128)S(1)}, s32[128]{0:T(128)}, u32[]{:S(2)}) copy-start(s32[128]{0:T(128)} %param.23) | copy-start | bytes 1540
  21.5 1.4 copy-start.17
  29.3 32.0 %all-to-all-start = ((bf16[32,80,128]{2,1,0:T(8,128)(2,1)}), bf16[32,80,128]{2,1,0:T(8,128)(2,1)S(1)}, u32[]{:S(2)}, u32[]{:S(2)}) async-start(bf16[32,80,128]{2,1,0:T(8,128)(2,1)} %get-tuple-element.32), calls=%async_computation | async-start | bytes 1310720 | tf_op jit(solution)/shard_map/all_to_all | solution.py:740
  39.0 8.8 %collective-permute-start.3 = (bf16[1,512,256]{2,1,0:T(8,128)(2,1)S(1)}, bf16[1,512,256]{2,1,0:T(8,128)(2,1)S(1)}, u32[]{:S(2)}, u32[]{:S(2)}) collective-permute-start(bf16[1,512,256]{2,1,0:T(8,128)(2,1)S(1)} %slice.19), channel_id=1, source_target_pairs={{0,192},{8,200},{16,208},{24,216},{32,224},{40,232},{48,240},{56,2... | collective-permute-start | bytes 786440 | tf_op jit(solution)/shard_map/ppermute | solution.py:747
  42.5 8.5 %collective-permute-start.2 = (bf16[1,512,256]{2,1,0:T(8,128)(2,1)S(1)}, bf16[1,512,256]{2,1,0:T(8,128)(2,1)S(1)}, u32[]{:S(2)}, u32[]{:S(2)}) collective-permute-start(bf16[1,512,256]{2,1,0:T(8,128)(2,1)S(1)} %slice.18), channel_id=1, source_target_pairs={{0,64},{8,72},{16,80},{24,88},{32,96},{40,104},{48,112},{56,120},{... | collective-permute-start | bytes 786440 | tf_op jit(solution)/shard_map/ppermute | solution.py:747
  69.7 34.4 %all-to-all-start.1 = ((bf16[32,64,128]{2,1,0:T(8,128)(2,1)}), bf16[32,64,128]{2,1,0:T(8,128)(2,1)}, u32[]{:S(2)}, u32[]{:S(2)}) async-start(bf16[32,64,128]{2,1,0:T(8,128)(2,1)} %copy-done.1), calls=%async_computation.1 | async-start | bytes 1048576 | tf_op jit(solution)/shard_map/all_to_all | solution.py:740
  78.0 81.2 %reduce-scatter.2.cloned.1.call-start = ((), (), s32[]{:S(2)}) async-start(), calls=%async_computation.5 | async-start | bytes 4718592 | tf_op jit(solution)/shard_map/reduce_scatter | solution.py:773
  90.1 4.6 %collective-permute-start.6 = (f32[5,8,512]{2,1,0:T(8,128)S(1)}, f32[5,8,512]{2,1,0:T(8,128)S(1)}, u32[]{:S(2)}, u32[]{:S(2)}) collective-permute-start(f32[5,8,512]{2,1,0:T(8,128)S(1)} %get-tuple-element.37), channel_id=1, source_target_pairs={{0,192},{8,200},{16,208},{24,216},{32,224},{40,232},{48,240},{56,2... | collective-permute-start | bytes 245768 | tf_op jit(solution)/shard_map/ppermute | solution.py:747
  93.0 4.9 %collective-permute-start.5 = (f32[5,8,512]{2,1,0:T(8,128)S(1)}, f32[5,8,512]{2,1,0:T(8,128)S(1)}, u32[]{:S(2)}, u32[]{:S(2)}) collective-permute-start(f32[5,8,512]{2,1,0:T(8,128)S(1)} %get-tuple-element.37), channel_id=1, source_target_pairs={{0,128},{8,136},{16,144},{24,152},{32,160},{40,168},{48,176},{56,1... | collective-permute-start | bytes 245768 | tf_op jit(solution)/shard_map/ppermute | solution.py:747
  93.0 5.4 %collective-permute-start.4 = (f32[5,8,512]{2,1,0:T(8,128)S(1)}, f32[5,8,512]{2,1,0:T(8,128)S(1)}, u32[]{:S(2)}, u32[]{:S(2)}) collective-permute-start(f32[5,8,512]{2,1,0:T(8,128)S(1)} %get-tuple-element.37), channel_id=1, source_target_pairs={{0,64},{8,72},{16,80},{24,88},{32,96},{40,104},{48,112},{56,120},{... | collective-permute-start | bytes 245768 | tf_op jit(solution)/shard_map/ppermute | solution.py:747
  104.1 1.2 copy-start.10
  104.1 1.5 copy-start.12
  107.4 1.6 copy-start.18
  109.0 19.5 %copy-start.8 = (s32[137]{0:T(256)S(1)}, s32[137]{0:T(256)}, u32[]{:S(2)}) copy-start(s32[137]{0:T(256)} %pad_add_fusion.listed) | copy-start | bytes 1648
  121.8 13.1 %all-to-all-start.3 = ((bf16[8,128,128]{2,1,0:T(8,128)(2,1)}), bf16[8,128,128]{2,1,0:T(8,128)(2,1)S(1)}, u32[]{:S(2)}, u32[]{:S(2)}) async-start(bf16[8,128,128]{2,1,0:T(8,128)(2,1)} %bitcast.20), calls=%async_computation.4 | async-start | bytes 524288 | tf_op jit(solution)/shard_map/all_to_all | solution.py:778
  128.5 2.2 %copy-start = (bf16[16,512,256]{2,1,0:T(8,128)(2,1)S(1)}, bf16[16,512,256]{2,1,0:T(8,128)(2,1)}, u32[]{:S(2)}) copy-start(bf16[16,512,256]{2,1,0:T(8,128)(2,1)} %all-gather.3.cloned.1.call-done) | copy-start | bytes 12582916
  135.0 18.8 %all-to-all-start.2 = ((bf16[4,512,256]{2,1,0:T(8,128)(2,1)}), bf16[4,512,256]{2,1,0:T(8,128)(2,1)S(1)}, u32[]{:S(2)}, u32[]{:S(2)}) async-start(bf16[4,512,256]{2,1,0:T(8,128)(2,1)} %far_queries.1), calls=%async_computation.2 | async-start | bytes 2097152 | tf_op jit(solution)/shard_map/all_to_all | solution.py:740
  159.2 1.0 copy-start.2
  (4 other events, 3.3 us)
Sparse Core Ops, SparseCore 0:
  10.2 73.1 all-gather.2
  104.3 54.8 reduce-scatter.1

commit v4 on v3

--- a/solution.py
+++ b/solution.py
@@ -68,7 +68,7 @@
 EMPTY = -1e30
 KINDS = 3
 FAR = NZ * SEG
-UNROLL = 4
+UNROLL = 8
 PAIR = 2 * HD
 
 

time: 169 us -> 169 us (level)
  no operation moved by 1% of the time
where the time goes in v4:
time: 169 us; the launch traced here: 168 us
  Pallas kernels  41.7 us (25%)
  starting transfers between devices  37.7 us (22%)
  waiting for transfers between devices  36.2 us (21%)
  local copies, waits for them, and re-layouts  20.7 us (12%)
  between operations  14.3 us (8%)
  blocking collectives  13.7 us (8%)
  other arithmetic  3.85 us (2%)
    all_to_all x3, starting transfers between devices, exchange(): lax.all_to_all(value, 'seq', 0, 0, tiled=True, axis_index_groups=groups)  20.4 us
    ppermute x7, waiting for transfers between devices, along_x(): return lax.ppermute(value, 'seq', pairs)  19 us
    unnamed x48, local copies, waits for them, and re-layouts  16.9 us
    all_gather x1, blocking collectives, per_device(): whole = lax.all_gather(part, 'head', tiled=True).astype(F32)  13.7 us
    pallas_call x1, Pallas kernels, scan_grads(): call(grads_body, 'scan_grads', [((TOK, WIDTH), BF16, vm), ((TOK, SH), F32...  12.8 us
    ppermute x7, starting transfers between devices, along_x(): return lax.ppermute(value, 'seq', pairs)  10.5 us
    all_to_all x3, waiting for transfers between devices, exchange(): lax.all_to_all(value, 'seq', 0, 0, tiled=True, axis_index_groups=groups)  10.3 us
    all_to_all x1, starting transfers between devices, per_device(): shares = lax.all_to_all(bc.reshape(8, 128, NST), 'head', 0, 0, tiled=True)  6.63 us
  transfers between devices with their start and end apart: 13, of which 11 were waited for; matrix products, arithmetic and copies ran while one was open for 5% of the time, Pallas kernels for 24%

profile of v4, /device:TPU:1, one launch (start us, length us, event | category | flops | bytes accessed | tf_op | source)
XLA Modules:
  0.0 168.1 jit_solution(17760008043162343246)
XLA Ops:
  12.2 3.4 %collective-permute-start.1 = (bf16[2,512,256]{2,1,0:T(8,128)(2,1)S(1)}, bf16[2,512,256]{2,1,0:T(8,128)(2,1)}, u32[]{:S(2)}, u32[]{:S(2)}) collective-permute-start(bf16[2,512,256]{2,1,0:T(8,128)(2,1)S(1)} %by_head.2.qo), channel_id=1, source_target_pairs={{0,192},{8,200},{16,208},{24,216},{32,224},{40,232},{48,240},{56,2... | collective-permute-start | bytes 1572872 | tf_op jit(solution)/shard_map/ppermute | solution.py:747
  15.7 1.2 copy-done.11
  16.9 4.6 %scan_ends.1 = (f32[4,1024,128]{2,1,0:T(8,128)S(1)}, f32[4,1024,128]{2,1,0:T(8,128)}, bf16[32,80,128]{2,1,0:T(8,128)(2,1)}) custom-call(bf16[512,1024]{1,0:T(8,128)(2,1)S(1)} %copy-done.9, bf16[512,1024]{1,0:T(8,128)(2,1)S(1)} %copy-done.11, f32[512,16]{1,0:T(8,128)S(1)} %copy.31.ld_ref, bf16[512,128]{1,0:T(8,128)(2,1)S(1)} %copy-done.13, ...), custom_call_target="tpu_custom_call" | custom-call | flops 1073741824 | bytes 8388608 | tf_op jit(solution)/shard_map/scan_ends/pallas_call | solution.py:602
  21.5 1.4 copy-done.17
  22.9 3.2 %collective-permute-done.1 = bf16[2,512,256]{2,1,0:T(8,128)(2,1)} collective-permute-done((bf16[2,512,256]{2,1,0:T(8,128)(2,1)S(1)}, bf16[2,512,256]{2,1,0:T(8,128)(2,1)}, u32[]{:S(2)}, u32[]{:S(2)}) %collective-permute-start.1) | collective-permute-done | bytes 524320 | tf_op jit(solution)/shard_map/ppermute | solution.py:747
  26.1 3.2 %collective-permute-done = bf16[2,512,256]{2,1,0:T(8,128)(2,1)} collective-permute-done((bf16[2,512,256]{2,1,0:T(8,128)(2,1)S(1)}, bf16[2,512,256]{2,1,0:T(8,128)(2,1)}, u32[]{:S(2)}, u32[]{:S(2)}) %collective-permute-start) | collective-permute-done | bytes 524320 | tf_op jit(solution)/shard_map/ppermute | solution.py:747
  29.3 8.6 %all-to-all-start = ((bf16[32,80,128]{2,1,0:T(8,128)(2,1)}), bf16[32,80,128]{2,1,0:T(8,128)(2,1)S(1)}, u32[]{:S(2)}, u32[]{:S(2)}) async-start(bf16[32,80,128]{2,1,0:T(8,128)(2,1)} %get-tuple-element.32), calls=%async_computation | async-start | bytes 1310720 | tf_op jit(solution)/shard_map/all_to_all | solution.py:740
  38.0 1.0 slice.19
  39.0 2.6 %collective-permute-start.3 = (bf16[1,512,256]{2,1,0:T(8,128)(2,1)S(1)}, bf16[1,512,256]{2,1,0:T(8,128)(2,1)S(1)}, u32[]{:S(2)}, u32[]{:S(2)}) collective-permute-start(bf16[1,512,256]{2,1,0:T(8,128)(2,1)S(1)} %slice.19), channel_id=1, source_target_pairs={{0,192},{8,200},{16,208},{24,216},{32,224},{40,232},{48,240},{56,2... | collective-permute-start | bytes 786440 | tf_op jit(solution)/shard_map/ppermute | solution.py:747
  41.6 1.0 slice.18
  42.9 4.9 %collective-permute-done.3 = bf16[1,512,256]{2,1,0:T(8,128)(2,1)S(1)} collective-permute-done((bf16[1,512,256]{2,1,0:T(8,128)(2,1)S(1)}, bf16[1,512,256]{2,1,0:T(8,128)(2,1)S(1)}, u32[]{:S(2)}, u32[]{:S(2)}) %collective-permute-start.3) | collective-permute-done | bytes 262176 | tf_op jit(solution)/shard_map/ppermute | solution.py:747
  47.8 3.2 %collective-permute-done.2 = bf16[1,512,256]{2,1,0:T(8,128)(2,1)S(1)} collective-permute-done((bf16[1,512,256]{2,1,0:T(8,128)(2,1)S(1)}, bf16[1,512,256]{2,1,0:T(8,128)(2,1)S(1)}, u32[]{:S(2)}, u32[]{:S(2)}) %collective-permute-start.2) | collective-permute-done | bytes 262176 | tf_op jit(solution)/shard_map/ppermute | solution.py:747
  51.0 10.3 %all-to-all-done.inp = bf16[32,80,128]{2,1,0:T(8,128)(2,1)S(1)} async-done(((bf16[32,80,128]{2,1,0:T(8,128)(2,1)}), bf16[32,80,128]{2,1,0:T(8,128)(2,1)S(1)}, u32[]{:S(2)}, u32[]{:S(2)}) %all-to-all-start) | async-done | bytes 655392 | tf_op jit(solution)/shard_map/all_to_all | solution.py:740
  62.8 2.0 %near_stats.1.near = f32[8,512]{1,0:T(8,128)S(1)} custom-call(bf16[2,512,256]{2,1,0:T(8,128)(2,1)S(1)} %by_head.2.qo, bf16[2,512,256]{2,1,0:T(8,128)(2,1)} %by_head.3.kv), custom_call_target="tpu_custom_call" | custom-call | flops 268435456 | bytes 1048576 | tf_op jit(solution)/shard_map/near_stats/pallas_call | solution.py:154
  65.1 1.3 pad_add_fusion.listed
  66.4 1.5 pad_maximum_fusion.qos
  69.7 8.3 %all-to-all-start.1 = ((bf16[32,64,128]{2,1,0:T(8,128)(2,1)}), bf16[32,64,128]{2,1,0:T(8,128)(2,1)}, u32[]{:S(2)}, u32[]{:S(2)}) async-start(bf16[32,64,128]{2,1,0:T(8,128)(2,1)} %copy-done.1), calls=%async_computation.1 | async-start | bytes 1048576 | tf_op jit(solution)/shard_map/all_to_all | solution.py:740
  78.0 5.3 %all-gather.3.cloned.1.call-done = bf16[16,512,256]{2,1,0:T(8,128)(2,1)} async-done(((bf16[2,512,256]{2,1,0:T(8,128)(2,1)}), bf16[16,512,256]{2,1,0:T(8,128)(2,1)}) %all-gather.3.cloned.1.call-update) | async-done | bytes 4194320 | tf_op jit(solution)/shard_map/all_gather | solution.py:757
  84.1 5.7 %far_stats.1 = (f32[5,8,512]{2,1,0:T(8,128)S(1)}, f32[72,8,256]{2,1,0:T(8,128)S(1)}, bf16[72,128,256]{2,1,0:T(8,128)(2,1)}, bf16[72,128,256]{2,1,0:T(8,128)(2,1)}) custom-call(s32[145]{0:T(256)S(1)} %copy-done.7, f32[8,512]{1,0:T(8,128)S(1)} %near_stats.1.near, bf16[8,2,512,256]{3,2,1,0:T(8,128)(2,1)} %bitcast.23, ...), custom_call_target="tpu_custom_call" | custom-call | flops 268435456 | bytes 6291456 | tf_op jit(solution)/shard_map/far_stats/pallas_call | solution.py:269
  89.8 3.3 %collective-permute-start.6 = (f32[5,8,512]{2,1,0:T(8,128)S(1)}, f32[5,8,512]{2,1,0:T(8,128)S(1)}, u32[]{:S(2)}, u32[]{:S(2)}) collective-permute-start(f32[5,8,512]{2,1,0:T(8,128)S(1)} %get-tuple-element.37), channel_id=1, source_target_pairs={{0,192},{8,200},{16,208},{24,216},{32,224},{40,232},{48,240},{56,2... | collective-permute-start | bytes 245768 | tf_op jit(solution)/shard_map/ppermute | solution.py:747
  94.6 3.4 %collective-permute-done.5 = f32[5,8,512]{2,1,0:T(8,128)S(1)} collective-permute-done((f32[5,8,512]{2,1,0:T(8,128)S(1)}, f32[5,8,512]{2,1,0:T(8,128)S(1)}, u32[]{:S(2)}, u32[]{:S(2)}) %collective-permute-start.5) | collective-permute-done | bytes 81952 | tf_op jit(solution)/shard_map/ppermute | solution.py:747
  98.8 5.5 %far_grads.1 = (bf16[8,1024,256]{2,1,0:T(8,128)(2,1)}, bf16[72,128,256]{2,1,0:T(8,128)(2,1)}) custom-call(s32[145]{0:T(256)S(1)} %copy-done.7, s32[1]{0:T(128)} %bitcast.me, f32[4,5,8,512]{3,2,1,0:T(8,128)S(1)} %pad_maximum_fusion.1.stats, f32[72,8,256]{2,1,0:T(8,128)S(1)} %get-tuple-element.38.highs, bf16[72,128,256]{2,1,0:T(8,128)(2,1)} %get-tuple-element.39.e_in, ...), custom_call_target="tpu_custom_call" | custom-call | flops 536870912 | bytes 12582912 | tf_op jit(solution)/shard_map/far_grads/pallas_call | solution.py:375
  104.3 1.2 copy-done.10
  107.6 1.6 copy-done.18
  109.2 12.8 %scan_grads.1 = (bf16[512,1024]{1,0:T(8,128)(2,1)}, f32[512,16]{1,0:T(8,128)S(1)}, bf16[1024,128]{1,0:T(8,128)(2,1)}) custom-call(bf16[512,1024]{1,0:T(8,128)(2,1)S(1)} %copy-done.10, bf16[512,1024]{1,0:T(8,128)(2,1)S(1)} %copy-done.12, f32[512,16]{1,0:T(8,128)S(1)} %copy.31.ld_ref, bf16[512,128]{1,0:T(8,128)(2,1)S(1)} %copy-done.14, ...), custom_call_target="tpu_custom_call" | custom-call | flops 4294967296 | bytes 12582912 | tf_op jit(solution)/shard_map/scan_grads/pallas_call | solution.py:719
  122.0 6.6 %all-to-all-start.3 = ((bf16[8,128,128]{2,1,0:T(8,128)(2,1)}), bf16[8,128,128]{2,1,0:T(8,128)(2,1)S(1)}, u32[]{:S(2)}, u32[]{:S(2)}) async-start(bf16[8,128,128]{2,1,0:T(8,128)(2,1)} %bitcast.20), calls=%async_computation.4 | async-start | bytes 524288 | tf_op jit(solution)/shard_map/all_to_all | solution.py:778
  128.7 2.2 %copy-done = bf16[16,512,256]{2,1,0:T(8,128)(2,1)S(1)} copy-done((bf16[16,512,256]{2,1,0:T(8,128)(2,1)S(1)}, bf16[16,512,256]{2,1,0:T(8,128)(2,1)}, u32[]{:S(2)}) %copy-start) | copy-done | bytes 4194328
  130.9 3.7 %far_queries.1 = bf16[4,512,256]{2,1,0:T(8,128)(2,1)} custom-call(s32[145]{0:T(256)S(1)} %copy-done.8, s32[1]{0:T(128)} %bitcast.me, bf16[72,128,256]{2,1,0:T(8,128)(2,1)} %get-tuple-element.41.ds_in, bf16[8,2,512,256]{3,2,1,0:T(8,128)(2,1)S(1)} %bitcast.24), custom_call_target="tpu_custom_call" | custom-call | flops 134217728 | bytes 6291456 | tf_op jit(solution)/shard_map/far_queries/pallas_call | solution.py:437
  135.2 3.5 %all-to-all-start.2 = ((bf16[4,512,256]{2,1,0:T(8,128)(2,1)}), bf16[4,512,256]{2,1,0:T(8,128)(2,1)S(1)}, u32[]{:S(2)}, u32[]{:S(2)}) async-start(bf16[4,512,256]{2,1,0:T(8,128)(2,1)} %far_queries.1), calls=%async_computation.2 | async-start | bytes 2097152 | tf_op jit(solution)/shard_map/all_to_all | solution.py:740
  139.4 13.7 %all_gather.11 = bf16[1024,128]{1,0:T(8,128)(2,1)S(1)} all-gather(bf16[128,128]{1,0:T(8,128)(2,1)S(1)} %reduce_sum.52), channel_id=1, replica_groups=mesh['seq'=32,'head'=8] {'head'}, dimensions={0}, use_global_device_ids=true | all-gather | bytes 294912 | tf_op jit(solution)/shard_map/all_gather | solution.py:781
  154.0 4.5 %near_grads.1 = (bf16[1024,128]{1,0:T(8,128)(2,1)}, f32[2,512,256]{2,1,0:T(8,128)S(1)}) custom-call(s32[1]{0:T(128)} %bitcast.me, f32[4,5,8,512]{3,2,1,0:T(8,128)S(1)} %pad_maximum_fusion.1.stats, bf16[2,512,256]{2,1,0:T(8,128)(2,1)S(1)} %by_head.2.qo, bf16[2,512,256]{2,1,0:T(8,128)(2,1)} %by_head.3.kv, bf16[4,512,256]{2,1,0:T(8,128)(2,1)S(1)} %all-to-all-done.2.dq_far), custom_call_target="tpu_custom_call" | custom-call | flops 671088640 | bytes 4194304 | tf_op jit(solution)/shard_map/near_grads/pallas_call | solution.py:484
  159.4 1.0 copy-done.2
  (79 shorter events, 18.2 us)
Async XLA Ops:
  7.2 76.2 %all-gather.3.cloned.1.call-start = ((), (), s32[]{:S(2)}) async-start(), calls=%async_computation.6 | async-start | bytes 4718592 | tf_op jit(solution)/shard_map/all_gather | solution.py:757
  7.2 1.0 copy-start.3
  8.2 0.9 copy-start.4
  9.1 6.4 %copy-start.19 = (f32[512,16]{0,1:T(8,128)S(1)}, f32[512,16]{0,1:T(8,128)}, u32[]{:S(2)}) copy-start(f32[512,16]{0,1:T(8,128)} %param.17) | copy-start | bytes 98308
  9.1 6.6 %copy-start.9 = (bf16[512,1024]{1,0:T(8,128)(2,1)S(1)}, bf16[512,1024]{1,0:T(8,128)(2,1)}, u32[]{:S(2)}) copy-start(bf16[512,1024]{1,0:T(8,128)(2,1)} %x_ref.3) | copy-start | bytes 3145732
  9.1 6.6 %copy-start.13 = (bf16[512,128]{1,0:T(8,128)(2,1)S(1)}, bf16[512,128]{1,0:T(8,128)(2,1)}, u32[]{:S(2)}) copy-start(bf16[512,128]{1,0:T(8,128)(2,1)} %b_ref.3) | copy-start | bytes 393220
  9.1 6.6 %copy-start.15 = (bf16[512,128]{1,0:T(8,128)(2,1)S(1)}, bf16[512,128]{1,0:T(8,128)(2,1)}, u32[]{:S(2)}) copy-start(bf16[512,128]{1,0:T(8,128)(2,1)} %c_ref.3) | copy-start | bytes 393220
  10.1 1.0 copy-start.5
  11.1 0.9 copy-start.6
  12.2 14.0 %collective-permute-start.1 = (bf16[2,512,256]{2,1,0:T(8,128)(2,1)S(1)}, bf16[2,512,256]{2,1,0:T(8,128)(2,1)}, u32[]{:S(2)}, u32[]{:S(2)}) collective-permute-start(bf16[2,512,256]{2,1,0:T(8,128)(2,1)S(1)} %by_head.2.qo), channel_id=1, source_target_pairs={{0,192},{8,200},{16,208},{24,216},{32,224},{40,232},{48,240},{56,2... | collective-permute-start | bytes 1572872 | tf_op jit(solution)/shard_map/ppermute | solution.py:747
  15.5 13.8 %collective-permute-start = (bf16[2,512,256]{2,1,0:T(8,128)(2,1)S(1)}, bf16[2,512,256]{2,1,0:T(8,128)(2,1)}, u32[]{:S(2)}, u32[]{:S(2)}) collective-permute-start(bf16[2,512,256]{2,1,0:T(8,128)(2,1)S(1)} %by_head.2.qo), channel_id=1, source_target_pairs={{0,64},{8,72},{16,80},{24,88},{32,96},{40,104},{48,112},{56,120},{... | collective-permute-start | bytes 1572872 | tf_op jit(solution)/shard_map/ppermute | solution.py:747
  15.7 1.2 copy-start.11
  16.9 21.0 %copy-start.20 = (s32[128,4]{0,1:T(4,128)S(1)}, s32[128,4]{0,1:T(4,128)}, u32[]{:S(2)}) copy-start(s32[128,4]{0,1:T(4,128)} %param.22) | copy-start | bytes 6148
  16.9 21.1 %copy-start.21 = (s32[128,4]{0,1:T(4,128)S(1)}, s32[128,4]{0,1:T(4,128)}, u32[]{:S(2)}) copy-start(s32[128,4]{0,1:T(4,128)} %param.21) | copy-start | bytes 6148
  16.9 21.1 %copy-start.22 = (s32[128]{0:T(128)S(1)}, s32[128]{0:T(128)}, u32[]{:S(2)}) copy-start(s32[128]{0:T(128)} %param.23) | copy-start | bytes 1540
  21.5 1.4 copy-start.17
  29.3 32.0 %all-to-all-start = ((bf16[32,80,128]{2,1,0:T(8,128)(2,1)}), bf16[32,80,128]{2,1,0:T(8,128)(2,1)S(1)}, u32[]{:S(2)}, u32[]{:S(2)}) async-start(bf16[32,80,128]{2,1,0:T(8,128)(2,1)} %get-tuple-element.32), calls=%async_computation | async-start | bytes 1310720 | tf_op jit(solution)/shard_map/all_to_all | solution.py:740
  39.0 8.8 %collective-permute-start.3 = (bf16[1,512,256]{2,1,0:T(8,128)(2,1)S(1)}, bf16[1,512,256]{2,1,0:T(8,128)(2,1)S(1)}, u32[]{:S(2)}, u32[]{:S(2)}) collective-permute-start(bf16[1,512,256]{2,1,0:T(8,128)(2,1)S(1)} %slice.19), channel_id=1, source_target_pairs={{0,192},{8,200},{16,208},{24,216},{32,224},{40,232},{48,240},{56,2... | collective-permute-start | bytes 786440 | tf_op jit(solution)/shard_map/ppermute | solution.py:747
  42.5 8.5 %collective-permute-start.2 = (bf16[1,512,256]{2,1,0:T(8,128)(2,1)S(1)}, bf16[1,512,256]{2,1,0:T(8,128)(2,1)S(1)}, u32[]{:S(2)}, u32[]{:S(2)}) collective-permute-start(bf16[1,512,256]{2,1,0:T(8,128)(2,1)S(1)} %slice.18), channel_id=1, source_target_pairs={{0,64},{8,72},{16,80},{24,88},{32,96},{40,104},{48,112},{56,120},{... | collective-permute-start | bytes 786440 | tf_op jit(solution)/shard_map/ppermute | solution.py:747
  69.7 34.6 %all-to-all-start.1 = ((bf16[32,64,128]{2,1,0:T(8,128)(2,1)}), bf16[32,64,128]{2,1,0:T(8,128)(2,1)}, u32[]{:S(2)}, u32[]{:S(2)}) async-start(bf16[32,64,128]{2,1,0:T(8,128)(2,1)} %copy-done.1), calls=%async_computation.1 | async-start | bytes 1048576 | tf_op jit(solution)/shard_map/all_to_all | solution.py:740
  78.0 81.4 %reduce-scatter.2.cloned.1.call-start = ((), (), s32[]{:S(2)}) async-start(), calls=%async_computation.5 | async-start | bytes 4718592 | tf_op jit(solution)/shard_map/reduce_scatter | solution.py:773
  89.8 4.8 %collective-permute-start.6 = (f32[5,8,512]{2,1,0:T(8,128)S(1)}, f32[5,8,512]{2,1,0:T(8,128)S(1)}, u32[]{:S(2)}, u32[]{:S(2)}) collective-permute-start(f32[5,8,512]{2,1,0:T(8,128)S(1)} %get-tuple-element.37), channel_id=1, source_target_pairs={{0,192},{8,200},{16,208},{24,216},{32,224},{40,232},{48,240},{56,2... | collective-permute-start | bytes 245768 | tf_op jit(solution)/shard_map/ppermute | solution.py:747
  93.1 4.9 %collective-permute-start.5 = (f32[5,8,512]{2,1,0:T(8,128)S(1)}, f32[5,8,512]{2,1,0:T(8,128)S(1)}, u32[]{:S(2)}, u32[]{:S(2)}) collective-permute-start(f32[5,8,512]{2,1,0:T(8,128)S(1)} %get-tuple-element.37), channel_id=1, source_target_pairs={{0,128},{8,136},{16,144},{24,152},{32,160},{40,168},{48,176},{56,1... | collective-permute-start | bytes 245768 | tf_op jit(solution)/shard_map/ppermute | solution.py:747
  93.6 5.2 %collective-permute-start.4 = (f32[5,8,512]{2,1,0:T(8,128)S(1)}, f32[5,8,512]{2,1,0:T(8,128)S(1)}, u32[]{:S(2)}, u32[]{:S(2)}) collective-permute-start(f32[5,8,512]{2,1,0:T(8,128)S(1)} %get-tuple-element.37), channel_id=1, source_target_pairs={{0,64},{8,72},{16,80},{24,88},{32,96},{40,104},{48,112},{56,120},{... | collective-permute-start | bytes 245768 | tf_op jit(solution)/shard_map/ppermute | solution.py:747
  104.3 1.2 copy-start.10
  104.3 1.5 copy-start.12
  107.6 1.6 copy-start.18
  109.2 19.4 %copy-start.8 = (s32[145]{0:T(256)S(1)}, s32[145]{0:T(256)}, u32[]{:S(2)}) copy-start(s32[145]{0:T(256)} %pad_add_fusion.listed) | copy-start | bytes 1744
  122.0 13.1 %all-to-all-start.3 = ((bf16[8,128,128]{2,1,0:T(8,128)(2,1)}), bf16[8,128,128]{2,1,0:T(8,128)(2,1)S(1)}, u32[]{:S(2)}, u32[]{:S(2)}) async-start(bf16[8,128,128]{2,1,0:T(8,128)(2,1)} %bitcast.20), calls=%async_computation.4 | async-start | bytes 524288 | tf_op jit(solution)/shard_map/all_to_all | solution.py:778
  128.7 2.2 %copy-start = (bf16[16,512,256]{2,1,0:T(8,128)(2,1)S(1)}, bf16[16,512,256]{2,1,0:T(8,128)(2,1)}, u32[]{:S(2)}) copy-start(bf16[16,512,256]{2,1,0:T(8,128)(2,1)} %all-gather.3.cloned.1.call-done) | copy-start | bytes 12582916
  135.2 18.8 %all-to-all-start.2 = ((bf16[4,512,256]{2,1,0:T(8,128)(2,1)}), bf16[4,512,256]{2,1,0:T(8,128)(2,1)S(1)}, u32[]{:S(2)}, u32[]{:S(2)}) async-start(bf16[4,512,256]{2,1,0:T(8,128)(2,1)} %far_queries.1), calls=%async_computation.2 | async-start | bytes 2097152 | tf_op jit(solution)/shard_map/all_to_all | solution.py:740
  159.4 1.0 copy-start.2
  (4 other events, 3.3 us)
Sparse Core Ops, SparseCore 0:
  10.2 73.1 all-gather.2
  104.4 54.9 reduce-scatter.1
